TPU v7x, 32 devices: a whole 2x2x4 slice. The times are simulated.
32 devices in a mesh: dp: 8 (over z, x), seq: 4 (over y, core).
Axes of the slice: x: 2, y: 2, z: 4, core: 2. Of those that a mesh axis runs over, the one named last changes fastest.
Arguments:
- tokens: bfloat16 [64, 512, 1024], P(('dp', 'seq')), may hold values from -6 to 6
- segments: int32 [64, 512], P(('dp', 'seq')), may hold values from 0 to 512, as said below
- cotangent: bfloat16 [64, 512, 1024], P(('dp', 'seq')), may hold values from -6 to 6
- w_qkv: bfloat16 [1024, 3072], P(('dp', 'seq')), may hold values from -0.1875 to 0.1875
- b_query: bfloat16 [1024], P(('dp', 'seq')), may hold values from -3 to 3
- b_value: bfloat16 [1024], P(('dp', 'seq')), may hold values from -3 to 3
- w_out: bfloat16 [1024, 1024], P(('dp', 'seq')), may hold values from -0.75 to 0.75
- b_out: bfloat16 [1024], P(('dp', 'seq')), may hold values from -3 to 3
- norm1_gain: bfloat16 [1024], P(('dp', 'seq')), may hold values from 0.5 to 1.5
- norm1_shift: bfloat16 [1024], P(('dp', 'seq')), may hold values from -3 to 3
- w_in: bfloat16 [1024, 4096], P(('dp', 'seq')), may hold values from -0.1875 to 0.1875
- b_in: bfloat16 [4096], P(('dp', 'seq')), may hold values from -3 to 3
- w_down: bfloat16 [4096, 1024], P(('dp', 'seq')), may hold values from -0.09375 to 0.09375
- b_down: bfloat16 [1024], P(('dp', 'seq')), may hold values from -3 to 3
- norm2_gain: bfloat16 [1024], P(('dp', 'seq')), may hold values from 0.5 to 1.5
- norm2_shift: bfloat16 [1024], P(('dp', 'seq')), may hold values from -3 to 3
Outputs:
- mixed: bfloat16 [64, 512, 1024], P(('dp', 'seq'))
- input_grad: float32 [64, 512, 1024], P(('dp', 'seq'))
- w_qkv_grad: float32 [1024, 3072], P(('dp', 'seq'))
- b_query_grad: float32 [1024], P(('dp', 'seq'))
- b_value_grad: float32 [1024], P(('dp', 'seq'))
- w_out_grad: float32 [1024, 1024], P(('dp', 'seq'))
- b_out_grad: float32 [1024], P(('dp', 'seq'))
- norm1_gain_grad: float32 [1024], P(('dp', 'seq'))
- norm1_shift_grad: float32 [1024], P(('dp', 'seq'))
- w_in_grad: float32 [1024, 4096], P(('dp', 'seq'))
- b_in_grad: float32 [4096], P(('dp', 'seq'))
- w_down_grad: float32 [4096, 1024], P(('dp', 'seq'))
- b_down_grad: float32 [1024], P(('dp', 'seq'))
- norm2_gain_grad: float32 [1024], P(('dp', 'seq'))
- norm2_shift_grad: float32 [1024], P(('dp', 'seq'))
Inputs may be any that keep to these rules, and one draw needn't show every extreme that they name: `segments`: segment numbers never fall along a sequence and start at 0; the last document of every sequence has number 512.
All inputs are finite; a program needn't handle non-finite values.
Results may differ from a plain program's by a relative error of at most 0.013.
The roundings to bfloat16 on the way count: a program that leaves them out, or rounds other values in their place, can miss the bound.
Values may be sent and summed in bfloat16 or wider, within the bound.
A program may use at most 256 MiB of HBM per device.

v0:
```python
import jax
import jax.numpy as jnp
from jax import lax
from jax.sharding import PartitionSpec as P

HEADS = 16
HEAD_DIM = 64


eps_norm = 1e-05


def layer_norm(hidden, gain, shift):
    center = hidden - jnp.mean(hidden, axis=-1, keepdims=True)
    spread = jnp.mean(center * center, axis=-1, keepdims=True)
    return center * lax.rsqrt(spread + eps_norm) * gain + shift


def gelu_exact(pre_gelu):
    return jax.nn.gelu(pre_gelu, approximate=False)


def product(left, right):
    return jnp.dot(left, right, preferred_element_type=jnp.float32)


def left_major(left, right):
    return lax.dot_general(
        left, right, (((0,), (0,)), ((), ())), preferred_element_type=jnp.float32
    )


def right_major(left, right):
    return lax.dot_general(
        left, right, (((1,), (1,)), ((), ())), preferred_element_type=jnp.float32
    )


def masked_scores(query_group, key_group, same_doc):
    scores = jnp.einsum(
        "sqge,skge->sgqk", query_group, key_group, preferred_element_type=jnp.float32
    ) * HEAD_DIM ** (-0.5)
    return jnp.where(same_doc[:, None], scores, -1e30)


def column_sums(matrix):
    return jnp.sum(matrix.astype(jnp.float32), axis=0)


def shards(
    tokens,
    segments,
    cotangent,
    w_qkv,
    b_query,
    b_value,
    w_out,
    b_out,
    norm1_gain,
    norm1_shift,
    w_in,
    b_in,
    w_down,
    b_down,
    norm2_gain,
    norm2_shift,
):
    gathered = (
        lax.all_gather(w_qkv, ("dp", "seq"), axis=0, tiled=True),
        lax.all_gather(b_query, ("dp", "seq"), axis=0, tiled=True),
        lax.all_gather(b_value, ("dp", "seq"), axis=0, tiled=True),
        lax.all_gather(w_out, ("dp", "seq"), axis=0, tiled=True),
        lax.all_gather(b_out, ("dp", "seq"), axis=0, tiled=True),
        lax.all_gather(norm1_gain, ("dp", "seq"), axis=0, tiled=True),
        lax.all_gather(norm1_shift, ("dp", "seq"), axis=0, tiled=True),
        lax.all_gather(w_in, ("dp", "seq"), axis=0, tiled=True),
        lax.all_gather(b_in, ("dp", "seq"), axis=0, tiled=True),
        lax.all_gather(w_down, ("dp", "seq"), axis=0, tiled=True),
        lax.all_gather(b_down, ("dp", "seq"), axis=0, tiled=True),
        lax.all_gather(norm2_gain, ("dp", "seq"), axis=0, tiled=True),
        lax.all_gather(norm2_shift, ("dp", "seq"), axis=0, tiled=True),
    )
    (
        full_qkv,
        full_bquery,
        full_bvalue,
        full_out,
        full_bout,
        full_gain_one,
        full_shift_one,
        full_in,
        full_bin,
        full_down,
        full_bdown,
        full_gain_two,
        full_shift_two,
    ) = gathered
    model_width = HEADS * HEAD_DIM
    seq_count = tokens.shape[0]
    seq_len = tokens.shape[1]
    tok_rows = seq_count * seq_len
    inputs = tokens.reshape(tok_rows, model_width)
    qkv_bias = jnp.concatenate([full_bquery, jnp.zeros_like(full_bquery), full_bvalue]).astype(
        jnp.float32
    )
    qkv = (product(inputs, full_qkv) + qkv_bias).astype(jnp.bfloat16)
    query_heads = qkv[:, :model_width].reshape(seq_count, seq_len, HEADS, HEAD_DIM)
    key_heads = qkv[:, model_width : 2 * model_width].reshape(seq_count, seq_len, HEADS, HEAD_DIM)
    value_heads = qkv[:, 2 * model_width :].reshape(seq_count, seq_len, HEADS, HEAD_DIM)
    same_doc = segments[:, :, None] == segments[:, None, :]
    group_size = 4
    head_starts = list(range(0, HEADS, group_size))
    attended_parts = []
    lse_parts = []
    for first_head in head_starts:
        head_pick = slice(first_head, first_head + group_size)
        scores = masked_scores(query_heads[:, :, head_pick], key_heads[:, :, head_pick], same_doc)
        row_peak = jnp.max(scores, axis=-1, keepdims=True)
        exp_scores = jnp.exp(scores - row_peak)
        row_total = jnp.sum(exp_scores, axis=-1, keepdims=True)
        probs_low = (exp_scores / row_total).astype(jnp.bfloat16)
        attended_parts.append(
            jnp.einsum(
                "sgqk,skge->sqge",
                probs_low,
                value_heads[:, :, head_pick],
                preferred_element_type=jnp.float32,
            )
        )
        lse_parts.append(row_peak + jnp.log(row_total))
    attended = (
        jnp.concatenate(attended_parts, axis=2).reshape(tok_rows, model_width).astype(jnp.bfloat16)
    )
    hidden_one = (
        inputs.astype(jnp.float32) + product(attended, full_out) + full_bout.astype(jnp.float32)
    )
    normed_one, norm_one_pull = jax.vjp(
        layer_norm,
        hidden_one,
        full_gain_one.astype(jnp.float32),
        full_shift_one.astype(jnp.float32),
    )
    normed_low = normed_one.astype(jnp.bfloat16)
    pre_gelu = product(normed_low, full_in) + full_bin.astype(jnp.float32)
    activated, gelu_pull = jax.vjp(gelu_exact, pre_gelu)
    act_low = activated.astype(jnp.bfloat16)
    hidden_two = normed_one + product(act_low, full_down) + full_bdown.astype(jnp.float32)
    mixed_full, norm_two_pull = jax.vjp(
        layer_norm,
        hidden_two,
        full_gain_two.astype(jnp.float32),
        full_shift_two.astype(jnp.float32),
    )
    mixed = mixed_full.astype(jnp.bfloat16).reshape(seq_count, seq_len, model_width)
    back_qkv, back_out, back_in, back_down = (
        lax.all_gather(w_qkv, ("dp", "seq"), axis=0, tiled=True),
        lax.all_gather(w_out, ("dp", "seq"), axis=0, tiled=True),
        lax.all_gather(w_in, ("dp", "seq"), axis=0, tiled=True),
        lax.all_gather(w_down, ("dp", "seq"), axis=0, tiled=True),
    )
    upstream = cotangent.reshape(tok_rows, model_width).astype(jnp.float32)
    grad_two, gain_two_grad, shift_two_grad = norm_two_pull(upstream)
    grad_two_low = grad_two.astype(jnp.bfloat16)
    down_grad = left_major(act_low, grad_two_low)
    down_bias_grad = column_sums(grad_two_low)
    (pre_grad,) = gelu_pull(right_major(grad_two_low, back_down))
    pre_low = pre_grad.astype(jnp.bfloat16)
    in_grad = left_major(normed_low, pre_low)
    in_bias_grad = column_sums(pre_low)
    normed_grad = right_major(pre_low, back_in) + grad_two
    grad_one, gain_one_grad, shift_one_grad = norm_one_pull(normed_grad)
    grad_one_low = grad_one.astype(jnp.bfloat16)
    out_grad = left_major(attended, grad_one_low)
    out_bias_grad = column_sums(grad_one_low)
    attended_grad = (
        right_major(grad_one_low, back_out)
        .astype(jnp.bfloat16)
        .reshape(seq_count, seq_len, HEADS, HEAD_DIM)
    )
    scale_factor = HEAD_DIM ** (-0.5)
    query_grads = []
    key_grads = []
    value_grads = []
    for index_group, first_head in enumerate(head_starts):
        head_pick = slice(first_head, first_head + group_size)
        scores = masked_scores(query_heads[:, :, head_pick], key_heads[:, :, head_pick], same_doc)
        soft_probs = jnp.exp(scores - lse_parts[index_group])
        probs_low = soft_probs.astype(jnp.bfloat16)
        prob_grad = jnp.einsum(
            "sqge,skge->sgqk",
            attended_grad[:, :, head_pick],
            value_heads[:, :, head_pick],
            preferred_element_type=jnp.float32,
        )
        inner_sum = jnp.sum(soft_probs * prob_grad, axis=-1, keepdims=True)
        score_low = (soft_probs * (prob_grad - inner_sum)).astype(jnp.bfloat16)
        query_grads.append(
            jnp.einsum(
                "sgqk,skge->sqge",
                score_low,
                key_heads[:, :, head_pick],
                preferred_element_type=jnp.float32,
            )
            * scale_factor
        )
        key_grads.append(
            jnp.einsum(
                "sgqk,sqge->skge",
                score_low,
                query_heads[:, :, head_pick],
                preferred_element_type=jnp.float32,
            )
            * scale_factor
        )
        value_grads.append(
            jnp.einsum(
                "sgqk,sqge->skge",
                probs_low,
                attended_grad[:, :, head_pick],
                preferred_element_type=jnp.float32,
            )
        )
    query_grad = jnp.concatenate(query_grads, axis=2).reshape(tok_rows, model_width)
    key_grad = jnp.concatenate(key_grads, axis=2).reshape(tok_rows, model_width)
    value_grad = jnp.concatenate(value_grads, axis=2).reshape(tok_rows, model_width)
    qkv_grad = jnp.concatenate([query_grad, key_grad, value_grad], axis=1).astype(jnp.bfloat16)
    qkv_weight_grad = left_major(inputs, qkv_grad)
    qkv_sums = column_sums(qkv_grad)
    input_grad = (right_major(qkv_grad, back_qkv) + grad_one).reshape(
        seq_count, seq_len, model_width
    )
    all_shards = (
        lax.psum_scatter(qkv_weight_grad, ("dp", "seq"), scatter_dimension=0, tiled=True),
        lax.psum_scatter(qkv_sums[:model_width], ("dp", "seq"), scatter_dimension=0, tiled=True),
        lax.psum_scatter(
            qkv_sums[2 * model_width :], ("dp", "seq"), scatter_dimension=0, tiled=True
        ),
        lax.psum_scatter(out_grad, ("dp", "seq"), scatter_dimension=0, tiled=True),
        lax.psum_scatter(out_bias_grad, ("dp", "seq"), scatter_dimension=0, tiled=True),
        lax.psum_scatter(gain_one_grad, ("dp", "seq"), scatter_dimension=0, tiled=True),
        lax.psum_scatter(shift_one_grad, ("dp", "seq"), scatter_dimension=0, tiled=True),
        lax.psum_scatter(in_grad, ("dp", "seq"), scatter_dimension=0, tiled=True),
        lax.psum_scatter(in_bias_grad, ("dp", "seq"), scatter_dimension=0, tiled=True),
        lax.psum_scatter(down_grad, ("dp", "seq"), scatter_dimension=0, tiled=True),
        lax.psum_scatter(down_bias_grad, ("dp", "seq"), scatter_dimension=0, tiled=True),
        lax.psum_scatter(gain_two_grad, ("dp", "seq"), scatter_dimension=0, tiled=True),
        lax.psum_scatter(shift_two_grad, ("dp", "seq"), scatter_dimension=0, tiled=True),
    )
    (
        qkv_shard,
        bquery_shard,
        bvalue_shard,
        out_shard,
        out_bias_shard,
        gain_one_shard,
        shift_one_shard,
        in_shard,
        in_bias_shard,
        down_shard,
        down_bias_shard,
        gain_two_shard,
        shift_two_shard,
    ) = all_shards
    return (
        mixed,
        input_grad,
        qkv_shard,
        bquery_shard,
        bvalue_shard,
        out_shard,
        out_bias_shard,
        gain_one_shard,
        shift_one_shard,
        in_shard,
        in_bias_shard,
        down_shard,
        down_bias_shard,
        gain_two_shard,
        shift_two_shard,
    )


def solution(mesh):
    in_specs = (
        P(("dp", "seq"), None, None),
        P(("dp", "seq"), None),
        P(("dp", "seq"), None, None),
        P(("dp", "seq"), None),
        P(("dp", "seq")),
        P(("dp", "seq")),
        P(("dp", "seq"), None),
        P(("dp", "seq")),
        P(("dp", "seq")),
        P(("dp", "seq")),
        P(("dp", "seq"), None),
        P(("dp", "seq")),
        P(("dp", "seq"), None),
        P(("dp", "seq")),
        P(("dp", "seq")),
        P(("dp", "seq")),
    )
    out_specs = (
        P(("dp", "seq"), None, None),
        P(("dp", "seq"), None, None),
        P(("dp", "seq"), None),
        P(("dp", "seq")),
        P(("dp", "seq")),
        P(("dp", "seq"), None),
        P(("dp", "seq")),
        P(("dp", "seq")),
        P(("dp", "seq")),
        P(("dp", "seq"), None),
        P(("dp", "seq")),
        P(("dp", "seq"), None),
        P(("dp", "seq")),
        P(("dp", "seq")),
        P(("dp", "seq")),
    )
    return jax.shard_map(shards, mesh=mesh, in_specs=in_specs, out_specs=out_specs, check_vma=False)
```

profile of v0, /device:TPU:0, one launch (start us, length us, event | category | flops | bytes accessed | tf_op | source)
XLA Modules:
  0.0 1100.2 jit_solution(9101159592264957507)
XLA Ops:
  16.7 42.4 %all-reduce.18 = (bf16[1024]{0:T(1024)(128)(2,1)S(1)}, bf16[1024]{0:T(1024)(128)(2,1)S(1)}, bf16[1024]{0:T(1024)(128)(2,1)S(1)}, bf16[1024]{0:T(1024)(128)(2,1)S...) all-reduce(bf16[1024]{0:T(1024)(128)(2,1)S(1)} %dynamic-update-slic, ...), channel_id=1, replica_groups=mesh['dp'=8,'seq'=4] {'dp','seq'}, use_global_device_ids=true, to_apply=%add.2 | all-reduce | flops 8192 | bytes 32768
  60.9 41.1 %all-gather = bf16[32,1,128]{2,1,0:T(2,128)(2,1)S(1)} all-gather(bf16[1,1,128]{2,1,0:T(2,128)(2,1)} %bitcast.186), channel_id=1, replica_groups=mesh['dp'=8,'seq'=4] {'dp','seq'}, dimensions={0}, use_global_device_ids=true | all-gather | bytes 8448 | tf_op jit(solution)/shard_map/all_gather | solution.py:77
  103.3 9.4 add_convert_fusion.1
  115.4 6.3 reshape.235
  121.7 5.6 fusion.94
  136.4 6.4 reshape.234
  142.8 5.6 fusion.95
  160.9 5.3 fusion.96
  195.8 5.2 fusion.79
  204.1 5.8 fusion.102
  215.0 5.5 all-gather.10.cloned.1.call-done
  220.5 51.7 %multiply_convert_fusion = (bf16[1024,4096]{1,0:T(8,128)(2,1)}, f32[1024,4096]{1,0:T(8,128)}, f32[1024,4096]{1,0:T(8,128)}) fusion(f32[4096]{0:T(1024)S(1)} %bitcast.184, bf16[1024,4096]{1,0:T(8,128)(2,1)} %all-gather.10.cloned.1.call-done, f32[1024,1024]{1,0:T(8,128)} %copy-done.7, f32[1024]{0:T(1024)S(1)} %convert_element_type.127, ...), kind=kOutput, calls=%fused_computation.4 | convolution fusion | flops 8872001536 | bytes 54558720 | tf_op jit(solution)/shard_map/dot_general | solution.py:24
  272.2 27.4 %all-gather.12.cloned.1.call-done = bf16[4096,1024]{1,0:T(8,128)(2,1)} async-done(((bf16[128,1024]{1,0:T(8,128)(2,1)}), bf16[4096,1024]{1,0:T(8,128)(2,1)}) %all-gather.12.cloned.1.call-update) | async-done | bytes 8388624 | tf_op jit(solution)/shard_map/all_gather | solution.py:78
  299.6 14.9 %fusion.103 = (f32[1024]{0:T(1024)S(1)}, f32[1024,1024]{1,0:T(8,128)S(1)}) fusion(f32[1024]{0:T(1024)S(1)} %copy-done.63, bf16[1024,4096]{1,0:T(8,128)(2,1)} %get-tuple-element.92, bf16[4096,1024]{1,0:T(8,128)(2,1)} %all-gather.12.cloned.1.call-done, f32[1024]{0:T(1024)S(1)} %convert_element_type.127, f32[1024]{0:T(1024)S(1)} %convert_element_type.126, ...), kind=kOutput, calls=%fused_computation.168 | convolution fusion | flops 8597273600 | bytes 25190400 | tf_op jit(solution)/shard_map/dot_general | solution.py:24
  324.0 24.8 %convert_reduce_fusion = (f32[4096]{0:T(1024)}, bf16[1024,4096]{1,0:T(8,128)(2,1)}) fusion(f32[1024,4096]{1,0:T(8,128)} %get-tuple-element.93, f32[1024,4096]{1,0:T(8,128)} %get-tuple-element.126, f32[4096]{0:T(1024)S(1)} %bitcast.185, bf16[1024,1024]{1,0:T(8,128)(2,1)S(1)} %get-tuple-element.83, bf16[4096,1024]{1,0:T(8,128)(2,1)} %all-gather.12.cloned.1.call-done), kind=kOutput, calls=%fused_computation.2 | convolution fusion | flops 8661233664 | bytes 52461568 | tf_op jit(solution)/shard_map/dot_general | solution.py:34
  348.8 17.5 %multiply_reduce_fusion.4 = (f32[1024]{0:T(1024)}, f32[1024]{0:T(1024)S(1)}, f32[1024]{0:T(1024)}, f32[1024,1024]{1,0:T(8,128)S(1)}) fusion(f32[1024,1024]{1,0:T(8,128)} %copy-done.7, f32[1024]{0:T(1024)S(1)} %fusion.83, f32[1024]{0:T(1024)S(1)} %broadcast_multiply_fusion.1, f32[1024]{0:T(1024)S(1)} %convert_element_type.126, f32[1024,1024]{1,0:T(8,128)} %copy-done.9, ...), kind=kOutput, calls=%fused_computation.67 | convolution fusion | flops 8600417280 | bytes 29388800 | tf_op jit(solution)/shard_map/dot_general | solution.py:34
  385.6 5.4 fusion.93
  392.7 5.7 fusion.76
  398.4 8.4 multiply_reduce_fusion.3
  408.4 5.6 fusion.70
  414.0 8.3 multiply_reduce_fusion.1
  424.2 7.4 multiply_convert_fusion.4
  460.9 6.3 multiply_reduce_fusion
  487.8 9.0 convolution_bitcast_fusion
  496.8 12.6 %copy.162 = f32[1024,3072]{1,0:T(8,128)} copy(f32[1024,3072]{0,1:T(8,128)} %convolution_bitcast_fusion) | data formatting | bytes 25165824
  510.1 16.9 %fusion.85 = f32[1024,4096]{1,0:T(8,128)} fusion(bf16[1024,4096]{1,0:T(8,128)(2,1)} %get-tuple-element.85, f32[1024,1024]{1,0:T(8,128)} %copy-done.7, f32[1024]{0:T(1024)S(1)} %copy-done.62, f32[1024]{0:T(1024)S(1)} %convert_element_type.126, f32[1024]{0:T(1024)S(1)} %fusion.83, f32[1024]{0:T(1024)S(1)} %broadcast_multiply_fusion.1), kind=kOutput, calls=%fused_computation.153 | convolution fusion | flops 8595177472 | bytes 29376512 | tf_op jit(solution)/shard_map/dot_general | solution.py:28
  528.6 14.7 %fusion.105 = f32[4096,1024]{1,0:T(8,128)} fusion(bf16[1024,4096]{1,0:T(8,128)(2,1)} %get-tuple-element.92, bf16[1024,1024]{1,0:T(8,128)(2,1)S(1)} %copy-done.36), kind=kOutput, calls=%fused_computation.170 | convolution fusion | flops 8589934592 | bytes 27262976 | tf_op jit(solution)/shard_map/dot_general | solution.py:28
  549.1 40.4 %all-reduce.17 = (f32[1024]{0:T(1024)S(1)}, f32[1024]{0:T(1024)S(1)}, f32[1024]{0:T(1024)S(1)}, f32[1024]{0:T(1024)S(1)}, f32[1024]{0:T(1024)S(1)}, /*index=5*/f...) all-reduce(f32[1024]{0:T(1024)S(1)} %get-tuple-element.115, ...), channel_id=3, replica_groups=mesh['dp'=8,'seq'=4] {'dp','seq'}, use_global_device_ids=true, to_apply=%region_22.23.clone | all-reduce | flops 12288 | bytes 98304
  594.8 13.4 %add_add_fusion.4 = f32[1024,1024]{1,0:T(8,128)} fusion(f32[1024,1024]{1,0:T(8,128)} %copy-done.6, f32[1024]{0:T(1024)S(1)} %copy-done.55, bf16[1024,3072]{0,1:T(8,128)(2,1)} %copy-done.10, bf16[1024,3072]{1,0:T(8,128)(2,1)} %all-gather.6.cloned.1.call-done), kind=kOutput, calls=%fused_computation.84 | convolution fusion | flops 6444548096 | bytes 20975616 | tf_op jit(solution)/shard_map/dot_general | solution.py:34
  608.2 112.2 %reduce-scatter.13.cloned.1.call-done = f32[32,3072]{1,0:T(8,128)} async-done(((f32[1024,3072]{1,0:T(8,128)}), f32[32,3072]{1,0:T(8,128)}) %reduce-scatter.13.cloned.1.call-update) | async-done | bytes 393232
  720.5 185.1 %reduce-scatter.9.cloned.1.call-done = f32[32,4096]{1,0:T(8,128)} async-done(((f32[1024,4096]{1,0:T(8,128)}), f32[32,4096]{1,0:T(8,128)}) %reduce-scatter.9.cloned.1.call-update) | async-done | bytes 524304 | tf_op jit(solution)/shard_map/reduce_scatter | solution.py:242
  905.6 187.6 %reduce-scatter.11.cloned.1.call-done = f32[128,1024]{1,0:T(8,128)} async-done(((f32[4096,1024]{1,0:T(8,128)}), f32[128,1024]{1,0:T(8,128)}) %reduce-scatter.11.cloned.1.call-update) | async-done | bytes 524304 | tf_op jit(solution)/shard_map/reduce_scatter | solution.py:244
  (282 shorter events, 170.7 us)
Async XLA Ops:
  7.2 96.1 %all-gather.6.cloned.1.call-start = ((), (), s32[]{:S(2)}) async-start(), calls=%async_computation.4 | async-start | bytes 6488064 | tf_op jit(solution)/shard_map/all_gather | solution.py:69
  7.9 196.2 %all-gather.8.cloned.1.call-start = ((), (), s32[]{:S(2)}) async-start(), calls=%async_computation.5 | async-start | bytes 2162688 | tf_op jit(solution)/shard_map/all_gather | solution.py:72
  8.7 211.8 %all-gather.10.cloned.1.call-start = ((), (), s32[]{:S(2)}) async-start(), calls=%async_computation.6 | async-start | bytes 8650752 | tf_op jit(solution)/shard_map/all_gather | solution.py:76
  9.4 290.1 %all-gather.12.cloned.1.call-start = ((), (), s32[]{:S(2)}) async-start(), calls=%async_computation.7 | async-start | bytes 8650752 | tf_op jit(solution)/shard_map/all_gather | solution.py:78
  10.0 598.2 %reduce-scatter.7.cloned.1.call-start = ((), (), s32[]{:S(2)}) async-start(), calls=%async_computation.8 | async-start | bytes 4325376 | tf_op jit(solution)/shard_map/reduce_scatter | solution.py:238
  59.1 240.4 %copy-start.61 = (f32[1024]{0:T(1024)}, f32[1024]{0:T(1024)S(1)}, u32[]{:S(2)}) copy-start(f32[1024]{0:T(1024)S(1)} %convert_element_type.127) | copy-start | bytes 12292
  154.5 24.2 %copy-start.11 = (bf16[2,512,4,64]{1,3,2,0:T(8,128)(2,1)}, bf16[2,512,4,64]{1,3,2,0:T(8,128)(2,1)S(1)}, u32[]{:S(2)}) copy-start(bf16[2,512,4,64]{1,3,2,0:T(8,128)(2,1)S(1)} %copy.176) | copy-start | bytes 1572868
  160.9 12.3 %copy-start.13 = (bf16[2,512,4,64]{1,3,2,0:T(8,128)(2,1)S(1)}, bf16[2,512,4,64]{1,3,2,0:T(8,128)(2,1)}, u32[]{:S(2)}) copy-start(bf16[2,512,4,64]{1,3,2,0:T(8,128)(2,1)} %copy.182) | copy-start | bytes 1572868
  160.9 12.3 %copy-start.19 = (bf16[2,512,4,64]{1,3,2,0:T(8,128)(2,1)S(1)}, bf16[2,512,4,64]{1,3,2,0:T(8,128)(2,1)}, u32[]{:S(2)}) copy-start(bf16[2,512,4,64]{1,3,2,0:T(8,128)(2,1)} %copy.183) | copy-start | bytes 1572868
  212.5 59.7 %copy-start.50 = (f32[1024]{0:T(1024)}, f32[1024]{0:T(1024)S(1)}, u32[]{:S(2)}) copy-start(f32[1024]{0:T(1024)S(1)} %multiply_reduce_fusion.7) | copy-start | bytes 12292
  220.5 79.0 %copy-start.63 = (f32[1024]{0:T(1024)S(1)}, f32[1024]{0:T(1024)}, u32[]{:S(2)}) copy-start(f32[1024]{0:T(1024)} %convert_element_type.131) | copy-start | bytes 12292
  299.5 15.5 %copy-start.4 = (bf16[2,512,1024]{2,1,0:T(8,128)(2,1)S(1)}, bf16[2,512,1024]{2,1,0:T(8,128)(2,1)}, u32[]{:S(2)}) copy-start(bf16[2,512,1024]{2,1,0:T(8,128)(2,1)} %param.18) | copy-start | bytes 6291460
  299.5 15.5 %copy-start.49 = (f32[1024]{0:T(1024)S(1)}, f32[1024]{0:T(1024)}, u32[]{:S(2)}) copy-start(f32[1024]{0:T(1024)} %convert_element_type.132) | copy-start | bytes 12292
  324.0 24.8 %copy-start.35 = (bf16[1024,1024]{1,0:T(8,128)(2,1)}, bf16[1024,1024]{1,0:T(8,128)(2,1)S(1)}, u32[]{:S(2)}) copy-start(bf16[1024,1024]{1,0:T(8,128)(2,1)S(1)} %get-tuple-element.83) | copy-start | bytes 6291460
  348.8 17.5 %copy-start.51 = (f32[1024]{0:T(1024)S(1)}, f32[1024]{0:T(1024)}, u32[]{:S(2)}) copy-start(f32[1024]{0:T(1024)} %copy-done.50) | copy-start | bytes 12292
  348.8 17.5 %copy-start.8 = (f32[1024,1024]{1,0:T(8,128)S(1)}, f32[1024,1024]{1,0:T(8,128)}, u32[]{:S(2)}) copy-start(f32[1024,1024]{1,0:T(8,128)} %copy-done.7) | copy-start | bytes 12582916
  385.6 7.0 copy-start.48
  391.0 7.3 copy-start.34
  398.4 10.0 copy-start.47
  406.8 7.3 copy-start.32
  422.4 298.1 %reduce-scatter.13.cloned.1.call-start = ((), (), s32[]{:S(2)}) async-start(), calls=%async_computation.11 | async-start | bytes 12976128
  424.2 9.1 copy-start.27
  424.2 14.1 %slice-start.2 = ((s8[8388608]{0:T(1024)(128)(4,1)}), s8[4194304]{0:T(1024)(128)(4,1)S(1)}, s32[]{:S(2)}) async-start(s8[8388608]{0:T(1024)(128)(4,1)} %bitcast.150), calls=%async_computation.14 | async-start | bytes 8388608
  424.2 7.4 copy-start.26
  424.2 9.0 copy-start.45
  424.2 14.1 %slice-start.3 = ((s8[8388608]{0:T(1024)(128)(4,1)}), s8[4194304]{0:T(1024)(128)(4,1)S(1)}, s32[]{:S(2)}) async-start(s8[8388608]{0:T(1024)(128)(4,1)} %bitcast.150), calls=%async_computation.15 | async-start | bytes 8388608
  431.6 6.7 copy-start.46
  433.3 6.5 slice-start.4
  450.0 10.9 slice-start
  509.5 396.1 %reduce-scatter.9.cloned.1.call-start = ((), (), s32[]{:S(2)}) async-start(), calls=%async_computation.9 | async-start | bytes 17301504 | tf_op jit(solution)/shard_map/reduce_scatter | solution.py:242
  527.1 566.1 %reduce-scatter.11.cloned.1.call-start = ((), (), s32[]{:S(2)}) async-start(), calls=%async_computation.10 | async-start | bytes 17301504 | tf_op jit(solution)/shard_map/reduce_scatter | solution.py:244
  543.4 51.4 %copy-start.55 = (f32[1024]{0:T(1024)S(1)}, f32[1024]{0:T(1024)}, u32[]{:S(2)}) copy-start(f32[1024]{0:T(1024)} %copy-done.54) | copy-start | bytes 12292
  (47 other events, 166.6 us)
Sparse Core Ops, SparseCore 0:
  10.9 72.4 all-gather.5
  86.3 54.8 all-gather.7
  144.1 76.3 all-gather.9
  223.2 76.2 all-gather.11
  422.5 139.8 reduce-scatter.6
  568.9 151.5 reduce-scatter.12
  723.4 182.0 reduce-scatter.8
  908.5 184.5 reduce-scatter.10
where the time goes:
time: 1110 us; the launch traced here: 1100 us
  waiting for transfers between devices  520 us (47%)
  matrix products  261 us (24%)
  local copies, waits for them, and re-layouts  131 us (12%)
  blocking collectives  124 us (11%)
  other arithmetic  48.2 us (4%)
  between operations  15.5 us (1%)
    reduce_scatter x1, waiting for transfers between devices, shards(): lax.psum_scatter(down_grad, ('dp', 'seq'), scatter_dimension=0, tiled=True)  188 us
    reduce_scatter x1, waiting for transfers between devices, shards(): lax.psum_scatter(in_grad, ('dp', 'seq'), scatter_dimension=0, tiled=True)  185 us
    unnamed x9, waiting for transfers between devices  115 us
    unnamed x2, blocking collectives  82.8 us
    dot_general x4, matrix products, product(): return jnp.dot(left, right, preferred_element_type=jnp.float32)  81.8 us
    unnamed x191, local copies, waits for them, and re-layouts  76.6 us
    dot_general x4, matrix products, right_major(): lax.dot_general(left, right, (((1,), (1,)), ((), ())), preferred_element_...  60.3 us
    dot_general x4, matrix products, left_major(): lax.dot_general(left, right, (((0,), (0,)), ((), ())), preferred_element_...  45 us
  transfers between devices with their start and end apart: 8, of which 5 were waited for; matrix products, arithmetic and copies ran while one was open for 28% of the time, Pallas kernels for 0%

commit v1 on v0

v1 whole, which is shorter than its diff:
```python
import jax
import jax.numpy as jnp
from jax import lax
from jax.experimental import pallas as pl
from jax.experimental.pallas import tpu as pltpu
from jax.sharding import PartitionSpec as P

HEADS = 16
HEAD_DIM = 64


eps_norm = 1e-05


def layer_norm(hidden, gain, shift):
    center = hidden - jnp.mean(hidden, axis=-1, keepdims=True)
    spread = jnp.mean(center * center, axis=-1, keepdims=True)
    return center * lax.rsqrt(spread + eps_norm) * gain + shift


def gelu_exact(pre_gelu):
    return jax.nn.gelu(pre_gelu, approximate=False)


def product(left, right):
    return jnp.dot(left, right, preferred_element_type=jnp.float32)


def left_major(left, right):
    return lax.dot_general(
        left, right, (((0,), (0,)), ((), ())), preferred_element_type=jnp.float32
    )


def right_major(left, right):
    return lax.dot_general(
        left, right, (((1,), (1,)), ((), ())), preferred_element_type=jnp.float32
    )


def column_sums(matrix):
    return jnp.sum(matrix.astype(jnp.float32), axis=0)


SCALE = HEAD_DIM ** (-0.5)
PAIR = 2 * HEAD_DIM


def head_mask(length, head):
    lanes = lax.broadcasted_iota(jnp.int32, (length, PAIR), 1)
    return (lanes >= head * HEAD_DIM) & (lanes < (head + 1) * HEAD_DIM)


def keep_head(block, mask):
    return jnp.where(mask, block, jnp.zeros_like(block))


def head_probs(query, key, same_doc):
    scores = jnp.where(same_doc, right_major(query, key) * SCALE, -1e30)
    exp_scores = jnp.exp(scores - jnp.max(scores, axis=-1, keepdims=True))
    return exp_scores * (1.0 / jnp.sum(exp_scores, axis=-1, keepdims=True))


def attend_kernel(seg_col, seg_row, query_ref, key_ref, value_ref, out_ref):
    same_doc = seg_col[0] == seg_row[0]
    query, key, value = query_ref[...], key_ref[...], value_ref[...]
    total = jnp.zeros(query.shape, jnp.float32)
    for head in range(2):
        mask = head_mask(query.shape[0], head)
        probs = head_probs(keep_head(query, mask), key, same_doc)
        total += product(probs.astype(jnp.bfloat16), keep_head(value, mask))
    out_ref[...] = total.astype(jnp.bfloat16)


def attend_back_kernel(seg_col, seg_row, query_ref, key_ref, value_ref, grad_ref, out_ref):
    same_doc = seg_col[0] == seg_row[0]
    query, key, value, grad = query_ref[...], key_ref[...], value_ref[...], grad_ref[...]
    query_grad = jnp.zeros(query.shape, jnp.float32)
    key_grad = jnp.zeros(query.shape, jnp.float32)
    value_grad = jnp.zeros(query.shape, jnp.float32)
    for head in range(2):
        mask = head_mask(query.shape[0], head)
        query_own, grad_own = keep_head(query, mask), keep_head(grad, mask)
        probs = head_probs(query_own, key, same_doc)
        prob_grad = right_major(grad_own, value)
        inner_sum = jnp.sum(probs * prob_grad, axis=-1, keepdims=True)
        score_low = (probs * (prob_grad - inner_sum)).astype(jnp.bfloat16)
        query_grad += product(score_low, keep_head(key, mask))
        key_grad += left_major(score_low, query_own)
        value_grad += left_major(probs.astype(jnp.bfloat16), grad_own)
    out_ref[0] = (query_grad * SCALE).astype(jnp.bfloat16)
    out_ref[1] = (key_grad * SCALE).astype(jnp.bfloat16)
    out_ref[2] = value_grad.astype(jnp.bfloat16)


def attention_specs(seq_len, pairs):
    def column_block(first):
        return pl.BlockSpec((seq_len, PAIR), lambda seq, pair: (seq, first + pair))

    return [
        pl.BlockSpec((1, seq_len, 1), lambda seq, pair: (seq, 0, 0)),
        pl.BlockSpec((1, 1, seq_len), lambda seq, pair: (seq, 0, 0)),
        column_block(0),
        column_block(pairs),
        column_block(2 * pairs),
        column_block(0),
    ]


def attend(segments, qkv):
    seq_count, seq_len = segments.shape
    pairs = HEADS // 2
    specs = attention_specs(seq_len, pairs)
    area = seq_count * HEADS * seq_len * seq_len
    return pl.pallas_call(
        attend_kernel,
        grid=(seq_count, pairs),
        in_specs=specs[:5],
        out_specs=specs[5],
        out_shape=jax.ShapeDtypeStruct((qkv.shape[0], HEADS * HEAD_DIM), jnp.bfloat16),
        compiler_params=pltpu.CompilerParams(vmem_limit_bytes=40 * 2**20),
        cost_estimate=pl.CostEstimate(
            flops=4 * PAIR * area, bytes_accessed=8 * qkv.size // 3, transcendentals=area
        ),
    )(segments[:, :, None], segments[:, None, :], qkv, qkv, qkv)


def attend_back(segments, qkv, attended_grad):
    seq_count, seq_len = segments.shape
    pairs = HEADS // 2
    specs = attention_specs(seq_len, pairs)
    area = seq_count * HEADS * seq_len * seq_len
    return pl.pallas_call(
        attend_back_kernel,
        grid=(seq_count, pairs),
        in_specs=specs,
        out_specs=pl.BlockSpec((3, seq_len, PAIR), lambda seq, pair: (0, seq, pair)),
        out_shape=jax.ShapeDtypeStruct((3, qkv.shape[0], HEADS * HEAD_DIM), jnp.bfloat16),
        compiler_params=pltpu.CompilerParams(vmem_limit_bytes=40 * 2**20),
        cost_estimate=pl.CostEstimate(
            flops=10 * PAIR * area, bytes_accessed=14 * qkv.size // 3, transcendentals=area
        ),
    )(segments[:, :, None], segments[:, None, :], qkv, qkv, qkv, attended_grad)


def scatter_rows(grad, swap):
    dp_size, seq_size = lax.axis_size("dp"), lax.axis_size("seq")
    dp_bits, seq_bits = dp_size.bit_length() - 1, seq_size.bit_length() - 1
    near = [("dp", 0)] + [("seq", bit) for bit in range(1, seq_bits)]
    if swap:
        near = near[::-1]
    order = [("seq", 0)] + near + [("dp", bit) for bit in range(dp_bits - 1, 0, -1)]
    width = grad.shape[1]
    left = [("dp", bit) for bit in range(dp_bits - 1, -1, -1)]
    left += [("seq", bit) for bit in range(seq_bits - 1, -1, -1)]
    part = grad.astype(jnp.bfloat16)
    for name, bit in order:
        place = left.index((name, bit))
        outer = 2**place
        left.remove((name, bit))
        view = part.reshape(outer, 2, -1, width)
        mine = (lax.axis_index(name) >> bit) & 1
        size = lax.axis_size(name)
        send = lax.dynamic_index_in_dim(view, 1 - mine, 1, keepdims=False)
        keep = lax.dynamic_index_in_dim(view, mine, 1, keepdims=False)
        came = lax.ppermute(send, name, [(i, i ^ (1 << bit)) for i in range(size)])
        total = keep.astype(jnp.float32) + came.astype(jnp.float32)
        part = total.astype(jnp.bfloat16) if left else total
    return part.reshape(-1, width)


def shards(
    tokens,
    segments,
    cotangent,
    w_qkv,
    b_query,
    b_value,
    w_out,
    b_out,
    norm1_gain,
    norm1_shift,
    w_in,
    b_in,
    w_down,
    b_down,
    norm2_gain,
    norm2_shift,
):
    rows = w_qkv.shape[0]
    vectors = (b_query, b_value, b_out, norm1_gain, norm1_shift, b_down, norm2_gain, norm2_shift)
    small = jnp.concatenate(
        [vector[:, None] for vector in vectors] + [b_in.reshape(rows, -1)], axis=1
    )
    small = jnp.pad(small, ((0, 0), (0, 128 - small.shape[1])))
    first = lax.all_gather(
        jnp.concatenate([w_qkv, small], axis=1), ("dp", "seq"), axis=0, tiled=True
    )
    full_out = lax.all_gather(w_out, ("dp", "seq"), axis=0, tiled=True)
    full_in = lax.all_gather(w_in, ("dp", "seq"), axis=0, tiled=True)
    full_down = lax.all_gather(w_down, ("dp", "seq"), axis=0, tiled=True)
    full_qkv = first[:, : w_qkv.shape[1]]
    small_full = first[:, w_qkv.shape[1] :]
    by_row = small_full[:, : len(vectors)].T
    (
        full_bquery,
        full_bvalue,
        full_bout,
        full_gain_one,
        full_shift_one,
        full_bdown,
        full_gain_two,
        full_shift_two,
    ) = [by_row[i] for i in range(len(vectors))]
    full_bin = small_full[:, len(vectors) : len(vectors) + b_in.shape[0] // rows].reshape(-1)
    model_width = HEADS * HEAD_DIM
    seq_count = tokens.shape[0]
    seq_len = tokens.shape[1]
    tok_rows = seq_count * seq_len
    inputs = tokens.reshape(tok_rows, model_width)
    qkv_bias = jnp.concatenate([full_bquery, jnp.zeros_like(full_bquery), full_bvalue]).astype(
        jnp.float32
    )
    qkv = (product(inputs, full_qkv) + qkv_bias).astype(jnp.bfloat16)
    attended = attend(segments, qkv)
    hidden_one = (
        inputs.astype(jnp.float32) + product(attended, full_out) + full_bout.astype(jnp.float32)
    )
    normed_one, norm_one_pull = jax.vjp(
        layer_norm,
        hidden_one,
        full_gain_one.astype(jnp.float32),
        full_shift_one.astype(jnp.float32),
    )
    normed_low = normed_one.astype(jnp.bfloat16)
    pre_gelu = product(normed_low, full_in) + full_bin.astype(jnp.float32)
    activated, gelu_pull = jax.vjp(gelu_exact, pre_gelu)
    act_low = activated.astype(jnp.bfloat16)
    hidden_two = normed_one + product(act_low, full_down) + full_bdown.astype(jnp.float32)
    mixed_full, norm_two_pull = jax.vjp(
        layer_norm,
        hidden_two,
        full_gain_two.astype(jnp.float32),
        full_shift_two.astype(jnp.float32),
    )
    mixed = mixed_full.astype(jnp.bfloat16).reshape(seq_count, seq_len, model_width)
    upstream = cotangent.reshape(tok_rows, model_width).astype(jnp.float32)
    grad_two, gain_two_grad, shift_two_grad = norm_two_pull(upstream)
    grad_two_low = grad_two.astype(jnp.bfloat16)
    down_grad = left_major(act_low, grad_two_low)
    down_bias_grad = column_sums(grad_two_low)
    (pre_grad,) = gelu_pull(right_major(grad_two_low, full_down))
    pre_low = pre_grad.astype(jnp.bfloat16)
    in_grad = left_major(normed_low, pre_low)
    in_bias_grad = column_sums(pre_low)
    normed_grad = right_major(pre_low, full_in) + grad_two
    grad_one, gain_one_grad, shift_one_grad = norm_one_pull(normed_grad)
    grad_one_low = grad_one.astype(jnp.bfloat16)
    out_grad = left_major(attended, grad_one_low)
    out_bias_grad = column_sums(grad_one_low)
    attended_grad = right_major(grad_one_low, full_out).astype(jnp.bfloat16)
    three = attend_back(segments, qkv, attended_grad)
    qkv_grad = jnp.concatenate([three[0], three[1], three[2]], axis=1)
    qkv_weight_grad = left_major(inputs, qkv_grad)
    qkv_sums = column_sums(qkv_grad)
    input_grad = (right_major(qkv_grad, full_qkv) + grad_one).reshape(
        seq_count, seq_len, model_width
    )
    sums = (
        qkv_sums[:model_width],
        qkv_sums[2 * model_width :],
        out_bias_grad,
        gain_one_grad,
        shift_one_grad,
        down_bias_grad,
        gain_two_grad,
        shift_two_grad,
    )
    small_grad = jnp.concatenate(
        [jnp.stack(sums), in_bias_grad.reshape(model_width, -1).T], axis=0
    )
    small_grad = jnp.pad(small_grad, ((0, 128 - small_grad.shape[0]), (0, 0))).T
    down_shard = scatter_rows(down_grad, False)
    in_shard = scatter_rows(in_grad, True)
    out_shard = scatter_rows(out_grad, False)
    half = qkv_weight_grad.shape[1] // 2
    qkv_shard = jnp.concatenate(
        [
            scatter_rows(qkv_weight_grad[:, :half], True),
            scatter_rows(qkv_weight_grad[:, half:], False),
        ],
        axis=1,
    )
    small_shard = scatter_rows(small_grad, True)
    columns = [small_shard[:, i] for i in range(len(vectors))]
    (
        bquery_shard,
        bvalue_shard,
        out_bias_shard,
        gain_one_shard,
        shift_one_shard,
        down_bias_shard,
        gain_two_shard,
        shift_two_shard,
    ) = columns
    in_bias_shard = small_shard[:, len(vectors) : len(vectors) + b_in.shape[0] // rows].reshape(-1)
    return (
        mixed,
        input_grad,
        qkv_shard,
        bquery_shard,
        bvalue_shard,
        out_shard,
        out_bias_shard,
        gain_one_shard,
        shift_one_shard,
        in_shard,
        in_bias_shard,
        down_shard,
        down_bias_shard,
        gain_two_shard,
        shift_two_shard,
    )


def solution(mesh):
    in_specs = (
        P(("dp", "seq"), None, None),
        P(("dp", "seq"), None),
        P(("dp", "seq"), None, None),
        P(("dp", "seq"), None),
        P(("dp", "seq")),
        P(("dp", "seq")),
        P(("dp", "seq"), None),
        P(("dp", "seq")),
        P(("dp", "seq")),
        P(("dp", "seq")),
        P(("dp", "seq"), None),
        P(("dp", "seq")),
        P(("dp", "seq"), None),
        P(("dp", "seq")),
        P(("dp", "seq")),
        P(("dp", "seq")),
    )
    out_specs = (
        P(("dp", "seq"), None, None),
        P(("dp", "seq"), None, None),
        P(("dp", "seq"), None),
        P(("dp", "seq")),
        P(("dp", "seq")),
        P(("dp", "seq"), None),
        P(("dp", "seq")),
        P(("dp", "seq")),
        P(("dp", "seq")),
        P(("dp", "seq"), None),
        P(("dp", "seq")),
        P(("dp", "seq"), None),
        P(("dp", "seq")),
        P(("dp", "seq")),
        P(("dp", "seq")),
    )
    return jax.shard_map(shards, mesh=mesh, in_specs=in_specs, out_specs=out_specs, check_vma=False)
```

time: 1110 us -> 732 us (0.66)
  waiting for transfers between devices: 520 us -> 330 us
  blocking collectives: 124 us -> 0 us
  local copies, waits for them, and re-layouts: 131 us -> 52.7 us
  matrix products: 261 us -> 183 us
  Pallas kernels: 0 us -> 73 us
  starting transfers between devices: 0.53 us -> 27.7 us
    reduce_scatter x3 -> x0, waiting for transfers between devices: 373 us -> none  [the longest x1 188 us: shards(): lax.psum_scatter(down_grad, ('dp', 'seq'), scatter_dimension=0, tiled=True)]
    ppermute x0 -> x30, waiting for transfers between devices: none -> 148 us  [scatter_rows(): came = lax.ppermute(send, name, [(i, i ^ 1 << bit) for i in range(size)])]
    all_gather x4, waiting for transfers between devices: 32.9 us -> 180 us  [the longest x1 72 us: shards(): full_in = lax.all_gather(w_in, ('dp', 'seq'), axis=0, tiled=True)]
    unnamed x9 -> x4, waiting for transfers between devices: 115 us -> 1.91 us
    unnamed x2 -> x0, blocking collectives: 82.8 us -> none
    dot_general x24 -> x0, matrix products: 73.9 us -> none  [the longest x4 28.2 us: shards(): jnp.einsum('sqge,skge->sgqk', attended_grad[:, :, head_pick], value_heads...]
    pallas_call x0 -> x2, Pallas kernels: none -> 73 us  [the longest x1 45.4 us: attend_back(): pl.pallas_call(attend_back_kernel, grid=(seq_count, pairs), in_specs=spec...]
    unnamed x191 -> x58, local copies, waits for them, and re-layouts: 76.6 us -> 13.6 us
  transfers between devices with their start and end apart: 8 -> 34, of which waited for: 5 -> 21; matrix products, arithmetic and copies ran while one was open for 28% -> 19% of each run, Pallas kernels for 0% -> 4%
where the time goes in v1:
time: 732 us; the launch traced here: 724 us
  waiting for transfers between devices  330 us (45%)
  matrix products  183 us (25%)
  Pallas kernels  73 us (10%)
  local copies, waits for them, and re-layouts  52.7 us (7%)
  other arithmetic  43.1 us (6%)
  starting transfers between devices  27.7 us (4%)
  between operations  14.9 us (2%)
    ppermute x30, waiting for transfers between devices, scatter_rows(): came = lax.ppermute(send, name, [(i, i ^ 1 << bit) for i in range(size)])  148 us
    dot_general x4, matrix products, product(): return jnp.dot(left, right, preferred_element_type=jnp.float32)  80.4 us
    all_gather x1, waiting for transfers between devices, shards(): full_in = lax.all_gather(w_in, ('dp', 'seq'), axis=0, tiled=True)  72 us
    all_gather x1, waiting for transfers between devices, shards(): lax.all_gather(jnp.concatenate([w_qkv, small], axis=1), ('dp', 'seq'), ax...  66.9 us
    dot_general x4, matrix products, right_major(): lax.dot_general(left, right, (((1,), (1,)), ((), ())), preferred_element_...  56.1 us
    dot_general x4, matrix products, left_major(): lax.dot_general(left, right, (((0,), (0,)), ((), ())), preferred_element_...  46 us
    pallas_call x1, Pallas kernels, attend_back(): pl.pallas_call(attend_back_kernel, grid=(seq_count, pairs), in_specs=spec...  45.4 us
    ppermute x30, starting transfers between devices, scatter_rows(): came = lax.ppermute(send, name, [(i, i ^ 1 << bit) for i in range(size)])  27.6 us
  transfers between devices with their start and end apart: 34, of which 21 were waited for; matrix products, arithmetic and copies ran while one was open for 19% of the time, Pallas kernels for 4%

profile of v1, /device:TPU:0, one launch (start us, length us, event | category | flops | bytes accessed | tf_op | source)
XLA Modules:
  0.0 724.3 jit_solution(15436383343952520570)
XLA Ops:
  22.3 66.9 %all-gather.5.cloned.1.call-done = bf16[1024,3200]{1,0:T(8,128)(2,1)} async-done(((bf16[32,3200]{1,0:T(8,128)(2,1)}), bf16[1024,3200]{1,0:T(8,128)(2,1)}) %all-gather.5.cloned.1.call-update) | async-done | bytes 6553616 | tf_op jit(solution)/shard_map/all_gather | solution.py:196
  93.4 9.4 %fusion.8.query_ref.key_ref.value_ref = bf16[1024,3072]{1,0:T(8,128)(2,1)S(1)} fusion(f32[3072]{0:T(1024)S(1)} %maximum_convert_fusion, bf16[1024,1024]{1,0:T(8,128)(2,1)} %bitcast.330, bf16[1024,3200]{1,0:T(8,128)(2,1)} %all-gather.5.cloned.1.call-done), kind=kOutput, calls=%fused_computation.24 | convolution fusion | flops 6448742400 | bytes 14692352 | tf_op jit(solution)/shard_map/dot_general | solution.py:26
  102.8 27.6 %shard_map.271 = bf16[1024,1024]{1,0:T(8,128)(2,1)S(1)} custom-call(s32[2,512,1]{2,1,0:T(8,128)S(1)} %copy.163.seg_col, s32[2,1,512]{2,1,0:T(1,128)S(1)} %broadcast_in_dim.60.seg_row, bf16[1024,3072]{1,0:T(8,128)(2,1)S(1)} %fusion.8.query_ref.key_ref.value_ref, bf16[1024,3072]{1,0:T(8,128)(2,1)S(1)} %fusion.8.query_ref.key_ref.value_ref, ...), custom_call_target="tpu_custom_call" | custom-call | flops 4294967296 | bytes 8388608 | tf_op jit(solution)/shard_map/pallas_call | solution.py:115
  133.0 14.0 %all-gather.7.cloned.1.call-done = bf16[1024,1024]{1,0:T(8,128)(2,1)} async-done(((bf16[32,1024]{1,0:T(8,128)(2,1)}), bf16[1024,1024]{1,0:T(8,128)(2,1)}) %all-gather.7.cloned.1.call-update) | async-done | bytes 2097168 | tf_op jit(solution)/shard_map/all_gather | solution.py:199
  147.0 4.7 fusion.65
  154.3 72.0 %all-gather.9.cloned.1.call-done = bf16[1024,4096]{1,0:T(8,128)(2,1)} async-done(((bf16[32,4096]{1,0:T(8,128)(2,1)}), bf16[1024,4096]{1,0:T(8,128)(2,1)}) %all-gather.9.cloned.1.call-update) | async-done | bytes 8388624 | tf_op jit(solution)/shard_map/all_gather | solution.py:200
  226.3 51.5 %multiply_convert_fusion = (bf16[1024,4096]{1,0:T(8,128)(2,1)}, f32[1024,4096]{1,0:T(8,128)}, f32[1024,4096]{1,0:T(8,128)}) fusion(f32[4096]{0:T(1024)S(1)} %reshape.508, bf16[1024,4096]{1,0:T(8,128)(2,1)} %all-gather.9.cloned.1.call-done, f32[1024,1024]{1,0:T(8,128)} %copy-done.6, f32[1024]{0:T(1024)S(1)} %get-tuple-element.23, ...), kind=kOutput, calls=%fused_computation.3 | convolution fusion | flops 8872001536 | bytes 54558720 | tf_op jit(solution)/shard_map/dot_general | solution.py:26
  277.8 27.4 %all-gather.11.cloned.1.call-done = bf16[4096,1024]{1,0:T(8,128)(2,1)} async-done(((bf16[128,1024]{1,0:T(8,128)(2,1)}), bf16[4096,1024]{1,0:T(8,128)(2,1)}) %all-gather.11.cloned.1.call-update) | async-done | bytes 8388624 | tf_op jit(solution)/shard_map/all_gather | solution.py:201
  305.2 14.8 %fusion.66 = (f32[1024]{0:T(1024)S(1)}, f32[1024,1024]{1,0:T(8,128)S(1)}) fusion(f32[1024]{0:T(1024)S(1)} %copy-done.23, bf16[1024,4096]{1,0:T(8,128)(2,1)} %get-tuple-element.46, bf16[4096,1024]{1,0:T(8,128)(2,1)} %all-gather.11.cloned.1.call-done, f32[1024]{0:T(1024)S(1)} %get-tuple-element.23, f32[1024]{0:T(1024)S(1)} %get-tuple-element.24, ...), kind=kOutput, calls=%fused_computation.188 | convolution fusion | flops 8597273600 | bytes 25190400 | tf_op jit(solution)/shard_map/dot_general | solution.py:26
  329.8 23.5 %fusion.57 = (bf16[4096]{0:T(1024)(128)(2,1)S(1)}, bf16[1024,4096]{1,0:T(8,128)(2,1)}) fusion(f32[1024,4096]{1,0:T(8,128)} %get-tuple-element.47, f32[1024,4096]{1,0:T(8,128)} %get-tuple-element.58, f32[4096]{0:T(1024)S(1)} %reshape.508, bf16[1024,1024]{1,0:T(8,128)(2,1)S(1)} %get-tuple-element.39, bf16[4096,1024]{1,0:T(8,128)(2,1)} %all-gather.11.cloned.1.call-done), kind=kOutput, calls=%fused_computation.180 | convolution fusion | flops 8657039360 | bytes 52453376 | tf_op jit(solution)/shard_map/dot_general | solution.py:36
  353.3 18.1 %multiply_reduce_fusion = (bf16[1024]{0:T(1024)(128)(2,1)S(1)}, f32[1024]{0:T(1024)S(1)}, bf16[1024]{0:T(1024)(128)(2,1)S(1)}, f32[1024,1024]{1,0:T(8,128)}) fusion(f32[1024,1024]{1,0:T(8,128)} %copy-done.6, f32[1024]{0:T(1024)S(1)} %fusion.51, f32[1024]{0:T(1024)S(1)} %broadcast_multiply_fusion.1, f32[1024]{0:T(1024)S(1)} %get-tuple-element.24, ...), kind=kOutput, calls=%fused_computation.44 | convolution fusion | flops 8600417280 | bytes 29384704 | tf_op jit(solution)/shard_map/dot_general | solution.py:36
  371.5 3.5 fusion.60
  380.5 45.4 %shard_map.272 = bf16[3,1024,1024]{2,1,0:T(8,128)(2,1)S(1)} custom-call(s32[2,512,1]{2,1,0:T(8,128)S(1)} %copy.163.seg_col, s32[2,1,512]{2,1,0:T(1,128)S(1)} %broadcast_in_dim.60.seg_row, bf16[1024,3072]{1,0:T(8,128)(2,1)} %copy-done, bf16[1024,3072]{1,0:T(8,128)(2,1)} %copy-done, bf16[1024,3072]{1,0:T(8,128)(2,1)} %copy-done, ...), custom_call_target="tpu_custom_call" | custom-call | flops 10737418240 | bytes 14680064 | tf_op jit(solution)/shard_map/pallas_call | solution.py:133
  426.7 12.5 %convert_bitcast_fusion = bf16[1024,3072]{1,0:T(8,128)(2,1)} fusion(bf16[1024,1024]{1,0:T(8,128)(2,1)} %bitcast.332, bf16[1024,1024]{1,0:T(8,128)(2,1)S(1)} %get-tuple-element.51, bf16[1024,1024]{1,0:T(8,128)(2,1)S(1)} %get-tuple-element.52, bf16[1024,1024]{1,0:T(8,128)(2,1)S(1)} %get-tuple-element.50), kind=kOutput, calls=%fused_computation.26 | convolution fusion | flops 6464471040 | bytes 14680064 | tf_op jit(solution)/shard_map/dot_general | solution.py:30
  441.4 3.8 convolution_convert_fusion.2
  445.1 15.0 %convolution_convert_fusion.1 = bf16[1024,4096]{1,0:T(8,128)(2,1)} fusion(bf16[1024,4096]{1,0:T(8,128)(2,1)} %get-tuple-element.37, f32[1024,1024]{1,0:T(8,128)S(1)} %copy-done.7, f32[1024]{0:T(1024)S(1)} %get-tuple-element.23, f32[1024]{0:T(1024)S(1)} %get-tuple-element.24, f32[1024]{0:T(1024)S(1)} %fusion.51, f32[1024]{0:T(1024)S(1)} %broadcast_multiply_fusion.1), kind=kOutput, calls=%fused_computation.23 | convolution fusion | flops 8599371776 | bytes 20987904 | tf_op jit(solution)/shard_map/dot_general | solution.py:30
  460.1 14.8 %convolution_convert_fusion = bf16[4096,1024]{1,0:T(8,128)(2,1)} fusion(bf16[1024,4096]{1,0:T(8,128)(2,1)} %get-tuple-element.46, bf16[1024,1024]{1,0:T(8,128)(2,1)S(1)} %get-tuple-element.39), kind=kOutput, calls=%fused_computation.22 | convolution fusion | flops 8594128896 | bytes 18874368 | tf_op jit(solution)/shard_map/dot_general | solution.py:30
  497.5 5.0 dynamic-slice_bitcast_fusion.1
  504.5 12.1 %add_add_fusion.4 = f32[1024,1024]{1,0:T(8,128)} fusion(f32[1024,1024]{1,0:T(8,128)S(1)} %copy-done.5, f32[1024]{0:T(1024)S(1)} %negate_multiply_fusion.1, bf16[1024,3200]{1,0:T(8,128)(2,1)} %all-gather.5.cloned.1.call-done, bf16[1024,1024]{1,0:T(8,128)(2,1)S(1)} %copy-done.13, bf16[1024,1024]{1,0:T(8,128)(2,1)} %copy-done.14, ...), kind=kOutput, calls=%fused_computation.52 | convolution fusion | flops 6463422464 | bytes 20975616 | tf_op jit(solution)/shard_map/dot_general | solution.py:36
  521.9 4.7 dynamic-slice_bitcast_fusion
  528.2 7.0 collective-permute-done.16
  559.6 12.6 %collective-permute-done.1 = bf16[8,32,1536]{2,1,0:T(8,128)(2,1)S(1)} collective-permute-done((bf16[8,32,1536]{2,1,0:T(8,128)(2,1)S(1)}, bf16[8,32,1536]{2,1,0:T(8,128)(2,1)S(1)}, u32[]{:S(2)}, u32[]{:S(2)}) %collective-permute-start.1) | collective-permute-done | bytes 786464 | tf_op jit(solution)/shard_map/ppermute | solution.py:166
  580.5 5.2 fusion.7
  589.6 5.8 collective-permute-done.3
  595.6 4.3 fusion.6
  601.5 25.8 %collective-permute-done.21 = bf16[8,32,4096]{2,1,0:T(8,128)(2,1)S(1)} collective-permute-done((bf16[8,32,4096]{2,1,0:T(8,128)(2,1)S(1)}, bf16[8,32,4096]{2,1,0:T(8,128)(2,1)S(1)}, u32[]{:S(2)}, u32[]{:S(2)}) %collective-permute-start.21) | collective-permute-done | bytes 2097184 | tf_op jit(solution)/shard_map/ppermute | solution.py:166
  629.1 19.6 %collective-permute-done.26 = bf16[4,256,1024]{2,1,0:T(8,128)(2,1)S(1)} collective-permute-done((bf16[4,256,1024]{2,1,0:T(8,128)(2,1)S(1)}, bf16[4,256,1024]{2,1,0:T(8,128)(2,1)S(1)}, u32[]{:S(2)}, u32[]{:S(2)}) %collective-permute-start.26) | collective-permute-done | bytes 2097184 | tf_op jit(solution)/shard_map/ppermute | solution.py:166
  651.2 12.7 %collective-permute-done.22 = bf16[4,32,4096]{2,1,0:T(8,128)(2,1)S(1)} collective-permute-done((bf16[4,32,4096]{2,1,0:T(8,128)(2,1)S(1)}, bf16[4,32,4096]{2,1,0:T(8,128)(2,1)S(1)}, u32[]{:S(2)}, u32[]{:S(2)}) %collective-permute-start.22) | collective-permute-done | bytes 1048608 | tf_op jit(solution)/shard_map/ppermute | solution.py:166
  668.4 26.8 %collective-permute-done.23 = bf16[1,64,4096]{2,1,0:T(8,128)(2,1)S(1)} collective-permute-done((bf16[1,64,4096]{2,1,0:T(8,128)(2,1)S(1)}, bf16[1,64,4096]{2,1,0:T(8,128)(2,1)S(1)}, u32[]{:S(2)}, u32[]{:S(2)}) %collective-permute-start.23) | collective-permute-done | bytes 524320 | tf_op jit(solution)/shard_map/ppermute | solution.py:166
  695.5 10.1 %collective-permute-done.28 = bf16[1,256,1024]{2,1,0:T(8,128)(2,1)S(1)} collective-permute-done((bf16[1,256,1024]{2,1,0:T(8,128)(2,1)S(1)}, bf16[1,256,1024]{2,1,0:T(8,128)(2,1)S(1)}, u32[]{:S(2)}, u32[]{:S(2)}) %collective-permute-start.28) | collective-permute-done | bytes 524320 | tf_op jit(solution)/shard_map/ppermute | solution.py:166
  705.8 5.3 collective-permute-done.24
  712.0 4.7 collective-permute-done.29
  (229 shorter events, 123.1 us)
Async XLA Ops:
  7.2 82.0 %all-gather.5.cloned.1.call-start = ((), (), s32[]{:S(2)}) async-start(), calls=%async_computation | async-start | bytes 6758400 | tf_op jit(solution)/shard_map/all_gather | solution.py:196
  15.8 131.2 %all-gather.7.cloned.1.call-start = ((), (), s32[]{:S(2)}) async-start(), calls=%async_computation.1 | async-start | bytes 2162688 | tf_op jit(solution)/shard_map/all_gather | solution.py:199
  16.5 209.8 %all-gather.9.cloned.1.call-start = ((), (), s32[]{:S(2)}) async-start(), calls=%async_computation.2 | async-start | bytes 8650752 | tf_op jit(solution)/shard_map/all_gather | solution.py:200
  17.3 287.9 %all-gather.11.cloned.1.call-start = ((), (), s32[]{:S(2)}) async-start(), calls=%async_computation.3 | async-start | bytes 8650752 | tf_op jit(solution)/shard_map/all_gather | solution.py:201
  478.3 59.0 %collective-permute-start.5 = (bf16[16,32,1536]{2,1,0:T(8,128)(2,1)}, bf16[16,32,1536]{2,1,0:T(8,128)(2,1)}, u32[]{:S(2)}, u32[]{:S(2)}) collective-permute-start(bf16[16,32,1536]{2,1,0:T(8,128)(2,1)} %dynamic-slice_bitcast_fusion.4), channel_id=1, source_target_pairs={{0,1},{1,0},{2,3},{3,2},{4,5},{5,4},{6,7},{7,6},{8,9},{9,8},{10,11... | collective-permute-start | bytes 4718600 | tf_op jit(solution)/shard_map/ppermute | solution.py:166
  491.3 54.8 %collective-permute-start = (bf16[16,32,1536]{2,1,0:T(8,128)(2,1)}, bf16[16,32,1536]{2,1,0:T(8,128)(2,1)}, u32[]{:S(2)}, u32[]{:S(2)}) collective-permute-start(bf16[16,32,1536]{2,1,0:T(8,128)(2,1)} %dynamic-slice_bitcast_fusion.5), channel_id=1, source_target_pairs={{0,1},{1,0},{2,3},{3,2},{4,5},{5,4},{6,7},{7,6},{8,9},{9,8},{10,11... | collective-permute-start | bytes 4718600 | tf_op jit(solution)/shard_map/ppermute | solution.py:166
  491.7 4.3 collective-permute-start.11
  493.3 24.2 %collective-permute-start.15 = (bf16[16,32,1024]{2,1,0:T(8,128)(2,1)S(1)}, bf16[16,32,1024]{2,1,0:T(8,128)(2,1)}, u32[]{:S(2)}, u32[]{:S(2)}) collective-permute-start(bf16[16,32,1024]{2,1,0:T(8,128)(2,1)S(1)} %dynamic-slice_bitcast_fusion.8), channel_id=1, source_target_pairs={{0,1},{1,0},{2,3},{3,2},{4,5},{5,4},{6,7},{7,6},{8,9},{9,8},{10,11... | collective-permute-start | bytes 3145736 | tf_op jit(solution)/shard_map/ppermute | solution.py:166
  496.1 6.5 collective-permute-start.12
  502.5 77.9 %collective-permute-start.20 = (bf16[16,32,4096]{2,1,0:T(8,128)(2,1)}, bf16[16,32,4096]{2,1,0:T(8,128)(2,1)}, u32[]{:S(2)}, u32[]{:S(2)}) collective-permute-start(bf16[16,32,4096]{2,1,0:T(8,128)(2,1)} %dynamic-slice_bitcast_fusion.1), channel_id=1, source_target_pairs={{0,1},{1,0},{2,3},{3,2},{4,5},{5,4},{6,7},{7,6},{8,9},{9,8},{10,11... | collective-permute-start | bytes 12582920 | tf_op jit(solution)/shard_map/ppermute | solution.py:166
  502.6 14.1 %collective-permute-start.13 = (bf16[1,64,128]{2,1,0:T(8,128)(2,1)S(1)}, bf16[1,64,128]{2,1,0:T(8,128)(2,1)S(1)}, u32[]{:S(2)}, u32[]{:S(2)}) collective-permute-start(bf16[1,64,128]{2,1,0:T(8,128)(2,1)S(1)} %dynamic-slice_bitcast_fusion.28), channel_id=1, source_target_pairs={{0,16},{4,20},{8,24},{12,28},{16,0},{20,4},{24,8},{28,12},{1,17},{... | collective-permute-start | bytes 49160 | tf_op jit(solution)/shard_map/ppermute | solution.py:166
  516.7 10.0 %collective-permute-start.14 = (bf16[1,32,128]{2,1,0:T(8,128)(2,1)S(1)}, bf16[1,32,128]{2,1,0:T(8,128)(2,1)S(1)}, u32[]{:S(2)}, u32[]{:S(2)}) collective-permute-start(bf16[1,32,128]{2,1,0:T(8,128)(2,1)S(1)} %fusion.50), channel_id=1, source_target_pairs={{0,8},{4,12},{8,0},{12,4},{16,24},{20,28},{24,16},{28,20},{1,9},{5... | collective-permute-start | bytes 24584 | tf_op jit(solution)/shard_map/ppermute | solution.py:166
  521.3 13.9 %collective-permute-start.16 = (bf16[4,64,1024]{2,1,0:T(8,128)(2,1)}, bf16[4,64,1024]{2,1,0:T(8,128)(2,1)}, u32[]{:S(2)}, u32[]{:S(2)}) collective-permute-start(bf16[4,64,1024]{2,1,0:T(8,128)(2,1)} %dynamic-slice_bitcast_fusion.13), channel_id=1, source_target_pairs={{0,4},{4,0},{8,12},{12,8},{16,20},{20,16},{24,28},{28,24},{1,5},{5... | collective-permute-start | bytes 1572872 | tf_op jit(solution)/shard_map/ppermute | solution.py:166
  526.7 68.9 %collective-permute-start.25 = (bf16[16,128,1024]{2,1,0:T(8,128)(2,1)}, bf16[16,128,1024]{2,1,0:T(8,128)(2,1)}, u32[]{:S(2)}, u32[]{:S(2)}) collective-permute-start(bf16[16,128,1024]{2,1,0:T(8,128)(2,1)} %dynamic-slice_bitcast_fusion), channel_id=1, source_target_pairs={{0,1},{1,0},{2,3},{3,2},{4,5},{5,4},{6,7},{7,6},{8,9},{9,8},{10,11... | collective-permute-start | bytes 12582920 | tf_op jit(solution)/shard_map/ppermute | solution.py:166
  536.7 7.1 collective-permute-start.17
  539.8 18.1 %collective-permute-start.6 = (bf16[4,64,1536]{2,1,0:T(8,128)(2,1)S(1)}, bf16[4,64,1536]{2,1,0:T(8,128)(2,1)S(1)}, u32[]{:S(2)}, u32[]{:S(2)}) collective-permute-start(bf16[4,64,1536]{2,1,0:T(8,128)(2,1)S(1)} %dynamic-slice_bitcast_fusion.9), channel_id=1, source_target_pairs={{0,4},{4,0},{8,12},{12,8},{16,20},{20,16},{24,28},{28,24},{1,5},{5... | collective-permute-start | bytes 2359304 | tf_op jit(solution)/shard_map/ppermute | solution.py:166
  543.9 7.3 %collective-permute-start.18 = (bf16[1,64,1024]{2,1,0:T(8,128)(2,1)S(1)}, bf16[1,64,1024]{2,1,0:T(8,128)(2,1)S(1)}, u32[]{:S(2)}, u32[]{:S(2)}) collective-permute-start(bf16[1,64,1024]{2,1,0:T(8,128)(2,1)S(1)} %dynamic-slice_bitcast_fusion.21), channel_id=1, source_target_pairs={{0,16},{4,20},{8,24},{12,28},{16,0},{20,4},{24,8},{28,12},{1,17},{... | collective-permute-start | bytes 393224 | tf_op jit(solution)/shard_map/ppermute | solution.py:166
  551.8 20.4 %collective-permute-start.1 = (bf16[8,32,1536]{2,1,0:T(8,128)(2,1)S(1)}, bf16[8,32,1536]{2,1,0:T(8,128)(2,1)S(1)}, u32[]{:S(2)}, u32[]{:S(2)}) collective-permute-start(bf16[8,32,1536]{2,1,0:T(8,128)(2,1)S(1)} %dynamic-slice_bitcast_fusion.10), channel_id=1, source_target_pairs={{0,2},{1,3},{2,0},{3,1},{4,6},{5,7},{6,4},{7,5},{8,10},{9,11},{10,... | collective-permute-start | bytes 2359304 | tf_op jit(solution)/shard_map/ppermute | solution.py:166
  558.1 18.3 %collective-permute-start.7 = (bf16[4,32,1536]{2,1,0:T(8,128)(2,1)S(1)}, bf16[4,32,1536]{2,1,0:T(8,128)(2,1)S(1)}, u32[]{:S(2)}, u32[]{:S(2)}) collective-permute-start(bf16[4,32,1536]{2,1,0:T(8,128)(2,1)S(1)} %dynamic-slice_bitcast_fusion.14), channel_id=1, source_target_pairs={{0,2},{1,3},{2,0},{3,1},{4,6},{5,7},{6,4},{7,5},{8,10},{9,11},{10,... | collective-permute-start | bytes 1179656 | tf_op jit(solution)/shard_map/ppermute | solution.py:166
  572.5 7.8 %collective-permute-start.2 = (bf16[4,32,1536]{2,1,0:T(8,128)(2,1)S(1)}, bf16[4,32,1536]{2,1,0:T(8,128)(2,1)S(1)}, u32[]{:S(2)}, u32[]{:S(2)}) collective-permute-start(bf16[4,32,1536]{2,1,0:T(8,128)(2,1)S(1)} %dynamic-slice_bitcast_fusion.15), channel_id=1, source_target_pairs={{0,4},{4,0},{8,12},{12,8},{16,20},{20,16},{24,28},{28,24},{1,5},{5... | collective-permute-start | bytes 1179656 | tf_op jit(solution)/shard_map/ppermute | solution.py:166
  576.6 12.4 %collective-permute-start.8 = (bf16[1,64,1536]{2,1,0:T(8,128)(2,1)S(1)}, bf16[1,64,1536]{2,1,0:T(8,128)(2,1)S(1)}, u32[]{:S(2)}, u32[]{:S(2)}) collective-permute-start(bf16[1,64,1536]{2,1,0:T(8,128)(2,1)S(1)} %dynamic-slice_bitcast_fusion.19), channel_id=1, source_target_pairs={{0,16},{4,20},{8,24},{12,28},{16,0},{20,4},{24,8},{28,12},{1,17},{... | collective-permute-start | bytes 589832 | tf_op jit(solution)/shard_map/ppermute | solution.py:166
  585.9 41.4 %collective-permute-start.21 = (bf16[8,32,4096]{2,1,0:T(8,128)(2,1)S(1)}, bf16[8,32,4096]{2,1,0:T(8,128)(2,1)S(1)}, u32[]{:S(2)}, u32[]{:S(2)}) collective-permute-start(bf16[8,32,4096]{2,1,0:T(8,128)(2,1)S(1)} %dynamic-slice_bitcast_fusion.3), channel_id=1, source_target_pairs={{0,2},{1,3},{2,0},{3,1},{4,6},{5,7},{6,4},{7,5},{8,10},{9,11},{10,... | collective-permute-start | bytes 6291464 | tf_op jit(solution)/shard_map/ppermute | solution.py:166
  586.8 8.6 %collective-permute-start.3 = (bf16[1,64,1536]{2,1,0:T(8,128)(2,1)S(1)}, bf16[1,64,1536]{2,1,0:T(8,128)(2,1)S(1)}, u32[]{:S(2)}, u32[]{:S(2)}) collective-permute-start(bf16[1,64,1536]{2,1,0:T(8,128)(2,1)S(1)} %dynamic-slice_bitcast_fusion.20), channel_id=1, source_target_pairs={{0,16},{4,20},{8,24},{12,28},{16,0},{20,4},{24,8},{28,12},{1,17},{... | collective-permute-start | bytes 589832 | tf_op jit(solution)/shard_map/ppermute | solution.py:166
  589.0 40.0 %collective-permute-start.9 = (bf16[1,32,1536]{2,1,0:T(8,128)(2,1)S(1)}, bf16[1,32,1536]{2,1,0:T(8,128)(2,1)S(1)}, u32[]{:S(2)}, u32[]{:S(2)}) collective-permute-start(bf16[1,32,1536]{2,1,0:T(8,128)(2,1)S(1)} %dynamic-slice_bitcast_fusion.23), channel_id=1, source_target_pairs={{0,8},{4,12},{8,0},{12,4},{16,24},{20,28},{24,16},{28,20},{1,9},{5... | collective-permute-start | bytes 294920 | tf_op jit(solution)/shard_map/ppermute | solution.py:166
  595.5 33.6 %collective-permute-start.4 = (bf16[1,32,1536]{2,1,0:T(8,128)(2,1)S(1)}, bf16[1,32,1536]{2,1,0:T(8,128)(2,1)S(1)}, u32[]{:S(2)}, u32[]{:S(2)}) collective-permute-start(bf16[1,32,1536]{2,1,0:T(8,128)(2,1)S(1)} %dynamic-slice_bitcast_fusion.24), channel_id=1, source_target_pairs={{0,8},{4,12},{8,0},{12,4},{16,24},{20,28},{24,16},{28,20},{1,9},{5... | collective-permute-start | bytes 294920 | tf_op jit(solution)/shard_map/ppermute | solution.py:166
  600.1 48.6 %collective-permute-start.26 = (bf16[4,256,1024]{2,1,0:T(8,128)(2,1)S(1)}, bf16[4,256,1024]{2,1,0:T(8,128)(2,1)S(1)}, u32[]{:S(2)}, u32[]{:S(2)}) collective-permute-start(bf16[4,256,1024]{2,1,0:T(8,128)(2,1)S(1)} %dynamic-slice_bitcast_fusion.2), channel_id=1, source_target_pairs={{0,4},{4,0},{8,12},{12,8},{16,20},{20,16},{24,28},{28,24},{1,5},{5... | collective-permute-start | bytes 6291464 | tf_op jit(solution)/shard_map/ppermute | solution.py:166
  628.4 35.5 %collective-permute-start.22 = (bf16[4,32,4096]{2,1,0:T(8,128)(2,1)S(1)}, bf16[4,32,4096]{2,1,0:T(8,128)(2,1)S(1)}, u32[]{:S(2)}, u32[]{:S(2)}) collective-permute-start(bf16[4,32,4096]{2,1,0:T(8,128)(2,1)S(1)} %dynamic-slice_bitcast_fusion.7), channel_id=1, source_target_pairs={{0,4},{4,0},{8,12},{12,8},{16,20},{20,16},{24,28},{28,24},{1,5},{5... | collective-permute-start | bytes 3145736 | tf_op jit(solution)/shard_map/ppermute | solution.py:166
  649.8 17.7 %collective-permute-start.27 = (bf16[4,128,1024]{2,1,0:T(8,128)(2,1)S(1)}, bf16[4,128,1024]{2,1,0:T(8,128)(2,1)S(1)}, u32[]{:S(2)}, u32[]{:S(2)}) collective-permute-start(bf16[4,128,1024]{2,1,0:T(8,128)(2,1)S(1)} %dynamic-slice_bitcast_fusion.6), channel_id=1, source_target_pairs={{0,2},{1,3},{2,0},{3,1},{4,6},{5,7},{6,4},{7,5},{8,10},{9,11},{10,... | collective-permute-start | bytes 3145736 | tf_op jit(solution)/shard_map/ppermute | solution.py:166
  664.1 31.1 %collective-permute-start.23 = (bf16[1,64,4096]{2,1,0:T(8,128)(2,1)S(1)}, bf16[1,64,4096]{2,1,0:T(8,128)(2,1)S(1)}, u32[]{:S(2)}, u32[]{:S(2)}) collective-permute-start(bf16[1,64,4096]{2,1,0:T(8,128)(2,1)S(1)} %dynamic-slice_bitcast_fusion.12), channel_id=1, source_target_pairs={{0,16},{4,20},{8,24},{12,28},{16,0},{20,4},{24,8},{28,12},{1,17},{... | collective-permute-start | bytes 1572872 | tf_op jit(solution)/shard_map/ppermute | solution.py:166
  668.0 37.5 %collective-permute-start.28 = (bf16[1,256,1024]{2,1,0:T(8,128)(2,1)S(1)}, bf16[1,256,1024]{2,1,0:T(8,128)(2,1)S(1)}, u32[]{:S(2)}, u32[]{:S(2)}) collective-permute-start(bf16[1,256,1024]{2,1,0:T(8,128)(2,1)S(1)} %dynamic-slice_bitcast_fusion.11), channel_id=1, source_target_pairs={{0,16},{4,20},{8,24},{12,28},{16,0},{20,4},{24,8},{28,12},{1,17},{... | collective-permute-start | bytes 1572872 | tf_op jit(solution)/shard_map/ppermute | solution.py:166
  695.4 15.7 %collective-permute-start.24 = (bf16[1,32,4096]{2,1,0:T(8,128)(2,1)S(1)}, bf16[1,32,4096]{2,1,0:T(8,128)(2,1)S(1)}, u32[]{:S(2)}, u32[]{:S(2)}) collective-permute-start(bf16[1,32,4096]{2,1,0:T(8,128)(2,1)S(1)} %dynamic-slice_bitcast_fusion.17), channel_id=1, source_target_pairs={{0,8},{4,12},{8,0},{12,4},{16,24},{20,28},{24,16},{28,20},{1,9},{5... | collective-permute-start | bytes 786440 | tf_op jit(solution)/shard_map/ppermute | solution.py:166
  705.8 10.9 %collective-permute-start.29 = (bf16[1,128,1024]{2,1,0:T(8,128)(2,1)S(1)}, bf16[1,128,1024]{2,1,0:T(8,128)(2,1)S(1)}, u32[]{:S(2)}, u32[]{:S(2)}) collective-permute-start(bf16[1,128,1024]{2,1,0:T(8,128)(2,1)S(1)} %dynamic-slice_bitcast_fusion.16), channel_id=1, source_target_pairs={{0,8},{4,12},{8,0},{12,4},{16,24},{20,28},{24,16},{28,20},{1,9},{5... | collective-permute-start | bytes 786440 | tf_op jit(solution)/shard_map/ppermute | solution.py:166
  (31 other events, 430.7 us)
Sparse Core Ops, SparseCore 0:
  15.9 73.2 all-gather.4
  92.0 54.8 all-gather.6
  149.8 76.4 all-gather.8
  229.0 76.1 all-gather.10

commit v2 on v1

--- a/solution.py
+++ b/solution.py
@@ -143,22 +143,26 @@
     )(segments[:, :, None], segments[:, None, :], qkv, qkv, qkv, attended_grad)
 
 
-def scatter_rows(grad, swap):
+def scatter_start(grad, swap):
     dp_size, seq_size = lax.axis_size("dp"), lax.axis_size("seq")
     dp_bits, seq_bits = dp_size.bit_length() - 1, seq_size.bit_length() - 1
     near = [("dp", 0)] + [("seq", bit) for bit in range(1, seq_bits)]
     if swap:
         near = near[::-1]
     order = [("seq", 0)] + near + [("dp", bit) for bit in range(dp_bits - 1, 0, -1)]
-    width = grad.shape[1]
     left = [("dp", bit) for bit in range(dp_bits - 1, -1, -1)]
     left += [("seq", bit) for bit in range(seq_bits - 1, -1, -1)]
-    part = grad.astype(jnp.bfloat16)
-    for name, bit in order:
+    return grad.astype(jnp.bfloat16), left, order
+
+
+def scatter_steps(state, steps):
+    part, left, order = state
+    left = list(left)
+    width = part.shape[-1]
+    for name, bit in order[:steps]:
         place = left.index((name, bit))
-        outer = 2**place
         left.remove((name, bit))
-        view = part.reshape(outer, 2, -1, width)
+        view = part.reshape(2**place, 2, -1, width)
         mine = (lax.axis_index(name) >> bit) & 1
         size = lax.axis_size(name)
         send = lax.dynamic_index_in_dim(view, 1 - mine, 1, keepdims=False)
@@ -166,7 +170,17 @@
         came = lax.ppermute(send, name, [(i, i ^ (1 << bit)) for i in range(size)])
         total = keep.astype(jnp.float32) + came.astype(jnp.float32)
         part = total.astype(jnp.bfloat16) if left else total
-    return part.reshape(-1, width)
+    return part, left, order[steps:]
+
+
+def scatter_end(state):
+    part = scatter_steps(state, len(state[2]))[0]
+    return part.reshape(-1, part.shape[-1])
+
+
+def tie(values, states):
+    values, parts = lax.optimization_barrier((values, [state[0] for state in states]))
+    return values, [(part,) + state[1:] for part, state in zip(parts, states)]
 
 
 def shards(
@@ -194,13 +208,13 @@
     )
     small = jnp.pad(small, ((0, 0), (0, 128 - small.shape[1])))
     first = lax.all_gather(
-        jnp.concatenate([w_qkv, small], axis=1), ("dp", "seq"), axis=0, tiled=True
-    )
-    full_out = lax.all_gather(w_out, ("dp", "seq"), axis=0, tiled=True)
+        jnp.concatenate([w_qkv, w_out, small], axis=1), ("dp", "seq"), axis=0, tiled=True
+    )
     full_in = lax.all_gather(w_in, ("dp", "seq"), axis=0, tiled=True)
     full_down = lax.all_gather(w_down, ("dp", "seq"), axis=0, tiled=True)
     full_qkv = first[:, : w_qkv.shape[1]]
-    small_full = first[:, w_qkv.shape[1] :]
+    full_out = first[:, w_qkv.shape[1] : w_qkv.shape[1] + w_out.shape[1]]
+    small_full = first[:, w_qkv.shape[1] + w_out.shape[1] :]
     by_row = small_full[:, : len(vectors)].T
     (
         full_bquery,
@@ -249,17 +263,28 @@
     grad_two_low = grad_two.astype(jnp.bfloat16)
     down_grad = left_major(act_low, grad_two_low)
     down_bias_grad = column_sums(grad_two_low)
+    (grad_two_low,), (down,) = tie((grad_two_low,), [scatter_start(down_grad, False)])
     (pre_grad,) = gelu_pull(right_major(grad_two_low, full_down))
     pre_low = pre_grad.astype(jnp.bfloat16)
+    in_bias_grad = column_sums(pre_low)
+    (pre_low,), (down,) = tie((pre_low,), [scatter_steps(down, 1)])
     in_grad = left_major(normed_low, pre_low)
-    in_bias_grad = column_sums(pre_low)
     normed_grad = right_major(pre_low, full_in) + grad_two
+    (normed_grad,), (down, inward) = tie(
+        (normed_grad,), [scatter_steps(down, 1), scatter_start(in_grad, True)]
+    )
     grad_one, gain_one_grad, shift_one_grad = norm_one_pull(normed_grad)
     grad_one_low = grad_one.astype(jnp.bfloat16)
     out_grad = left_major(attended, grad_one_low)
     out_bias_grad = column_sums(grad_one_low)
     attended_grad = right_major(grad_one_low, full_out).astype(jnp.bfloat16)
+    (attended_grad,), (inward, outward) = tie(
+        (attended_grad,), [scatter_steps(inward, 1), scatter_start(out_grad, False)]
+    )
     three = attend_back(segments, qkv, attended_grad)
+    (three,), (down, inward, outward) = tie(
+        (three,), [scatter_steps(down, 2), scatter_steps(inward, 1), scatter_steps(outward, 1)]
+    )
     qkv_grad = jnp.concatenate([three[0], three[1], three[2]], axis=1)
     qkv_weight_grad = left_major(inputs, qkv_grad)
     qkv_sums = column_sums(qkv_grad)
@@ -280,18 +305,18 @@
         [jnp.stack(sums), in_bias_grad.reshape(model_width, -1).T], axis=0
     )
     small_grad = jnp.pad(small_grad, ((0, 128 - small_grad.shape[0]), (0, 0))).T
-    down_shard = scatter_rows(down_grad, False)
-    in_shard = scatter_rows(in_grad, True)
-    out_shard = scatter_rows(out_grad, False)
+    down_shard = scatter_end(down)
+    in_shard = scatter_end(inward)
+    out_shard = scatter_end(outward)
     half = qkv_weight_grad.shape[1] // 2
     qkv_shard = jnp.concatenate(
         [
-            scatter_rows(qkv_weight_grad[:, :half], True),
-            scatter_rows(qkv_weight_grad[:, half:], False),
+            scatter_end(scatter_start(qkv_weight_grad[:, :half], True)),
+            scatter_end(scatter_start(qkv_weight_grad[:, half:], False)),
         ],
         axis=1,
     )
-    small_shard = scatter_rows(small_grad, True)
+    small_shard = scatter_end(scatter_start(small_grad, True))
     columns = [small_shard[:, i] for i in range(len(vectors))]
     (
         bquery_shard,

time: 732 us -> 680 us (0.929)
  waiting for transfers between devices: 330 us -> 266 us
  matrix products: 183 us -> 174 us
  other arithmetic: 43.1 us -> 51.9 us
  local copies, waits for them, and re-layouts: 52.7 us -> 61.3 us
    all_gather x1, waiting for transfers between devices: 72 us -> 30.3 us  [shards(): full_in = lax.all_gather(w_in, ('dp', 'seq'), axis=0, tiled=True)]
    ppermute x30, waiting for transfers between devices: 148 us -> 128 us  [scatter_steps(): came = lax.ppermute(send, name, [(i, i ^ 1 << bit) for i in range(size)])]
    dot_general x4, matrix products: 46 us -> 38 us  [left_major(): lax.dot_general(left, right, (((0,), (0,)), ((), ())), preferred_element_...]
    all_gather x2 -> x1, waiting for transfers between devices: 80.8 us -> 78.1 us  [shards(): lax.all_gather(jnp.concatenate([w_qkv, w_out, small], axis=1), ('dp', 'se...]
    unnamed x58 -> x76, local copies, waits for them, and re-layouts: 13.6 us -> 15.9 us
  transfers between devices with their start and end apart: 34 -> 33, of which waited for: 21 -> 20; matrix products, arithmetic and copies ran while one was open for 19% -> 29% of each run, Pallas kernels for 4% -> 11%
where the time goes in v2:
time: 680 us; the launch traced here: 673 us
  waiting for transfers between devices  266 us (39%)
  matrix products  174 us (26%)
  Pallas kernels  73.3 us (11%)
  local copies, waits for them, and re-layouts  61.3 us (9%)
  other arithmetic  51.9 us (8%)
  starting transfers between devices  31.1 us (5%)
  between operations  15.2 us (2%)
    ppermute x30, waiting for transfers between devices, scatter_steps(): came = lax.ppermute(send, name, [(i, i ^ 1 << bit) for i in range(size)])  128 us
    dot_general x4, matrix products, product(): return jnp.dot(left, right, preferred_element_type=jnp.float32)  80.5 us
    all_gather x1, waiting for transfers between devices, shards(): lax.all_gather(jnp.concatenate([w_qkv, w_out, small], axis=1), ('dp', 'se...  78.1 us
    dot_general x4, matrix products, right_major(): lax.dot_general(left, right, (((1,), (1,)), ((), ())), preferred_element_...  55.5 us
    pallas_call x1, Pallas kernels, attend_back(): pl.pallas_call(attend_back_kernel, grid=(seq_count, pairs), in_specs=spec...  45.8 us
    dot_general x4, matrix products, left_major(): lax.dot_general(left, right, (((0,), (0,)), ((), ())), preferred_element_...  38 us
    ppermute x30, starting transfers between devices, scatter_steps(): came = lax.ppermute(send, name, [(i, i ^ 1 << bit) for i in range(size)])  31 us
    all_gather x1, waiting for transfers between devices, shards(): full_in = lax.all_gather(w_in, ('dp', 'seq'), axis=0, tiled=True)  30.3 us
  transfers between devices with their start and end apart: 33, of which 20 were waited for; matrix products, arithmetic and copies ran while one was open for 29% of the time, Pallas kernels for 11%

profile of v2, /device:TPU:0, one launch (start us, length us, event | category | flops | bytes accessed | tf_op | source)
XLA Modules:
  0.0 672.6 jit_solution(3838029399469856419)
XLA Ops:
  18.9 78.1 %all-gather.4.cloned.1.call-done = bf16[1024,4224]{1,0:T(8,128)(2,1)} async-done(((bf16[32,4224]{1,0:T(8,128)(2,1)}), bf16[1024,4224]{1,0:T(8,128)(2,1)}) %all-gather.4.cloned.1.call-update) | async-done | bytes 8650768 | tf_op jit(solution)/shard_map/all_gather | solution.py:210
  101.3 9.4 %fusion.8.query_ref.key_ref.value_ref = bf16[1024,3072]{1,0:T(8,128)(2,1)S(1)} fusion(f32[3072]{0:T(1024)S(1)} %maximum_convert_fusion, bf16[1024,1024]{1,0:T(8,128)(2,1)} %bitcast.326, bf16[1024,4224]{1,0:T(8,128)(2,1)} %all-gather.4.cloned.1.call-done), kind=kOutput, calls=%fused_computation.24 | convolution fusion | flops 6448742400 | bytes 14692352 | tf_op jit(solution)/shard_map/dot_general | solution.py:26
  110.7 27.6 %shard_map.271 = bf16[1024,1024]{1,0:T(8,128)(2,1)S(1)} custom-call(s32[2,512,1]{2,1,0:T(8,128)S(1)} %copy.163.seg_col, s32[2,1,512]{2,1,0:T(1,128)S(1)} %broadcast_in_dim.60.seg_row, bf16[1024,3072]{1,0:T(8,128)(2,1)S(1)} %fusion.8.query_ref.key_ref.value_ref, bf16[1024,3072]{1,0:T(8,128)(2,1)S(1)} %fusion.8.query_ref.key_ref.value_ref, ...), custom_call_target="tpu_custom_call" | custom-call | flops 4294967296 | bytes 8388608 | tf_op jit(solution)/shard_map/pallas_call | solution.py:115
  138.3 4.9 fusion.67
  145.8 30.3 %all-gather.6.cloned.1.call-done = bf16[1024,4096]{1,0:T(8,128)(2,1)} async-done(((bf16[32,4096]{1,0:T(8,128)(2,1)}), bf16[1024,4096]{1,0:T(8,128)(2,1)}) %all-gather.6.cloned.1.call-update) | async-done | bytes 8388624 | tf_op jit(solution)/shard_map/all_gather | solution.py:213
  176.1 51.4 %multiply_convert_fusion = (bf16[1024,4096]{1,0:T(8,128)(2,1)}, f32[1024,4096]{1,0:T(8,128)}, f32[1024,4096]{1,0:T(8,128)}) fusion(f32[4096]{0:T(1024)S(1)} %reshape.508, bf16[1024,4096]{1,0:T(8,128)(2,1)} %all-gather.6.cloned.1.call-done, f32[1024,1024]{1,0:T(8,128)} %copy-done.3, f32[1024]{0:T(1024)S(1)} %get-tuple-element.51, ...), kind=kOutput, calls=%fused_computation.3 | convolution fusion | flops 8872001536 | bytes 54558720 | tf_op jit(solution)/shard_map/dot_general | solution.py:26
  227.6 27.6 %all-gather.8.cloned.1.call-done = bf16[4096,1024]{1,0:T(8,128)(2,1)} async-done(((bf16[128,1024]{1,0:T(8,128)(2,1)}), bf16[4096,1024]{1,0:T(8,128)(2,1)}) %all-gather.8.cloned.1.call-update) | async-done | bytes 8388624 | tf_op jit(solution)/shard_map/all_gather | solution.py:214
  255.2 14.8 %fusion.68 = (f32[1024]{0:T(1024)S(1)}, f32[1024,1024]{1,0:T(8,128)S(1)}) fusion(f32[1024]{0:T(1024)S(1)} %copy-done.31, bf16[1024,4096]{1,0:T(8,128)(2,1)} %get-tuple-element.74, bf16[4096,1024]{1,0:T(8,128)(2,1)} %all-gather.8.cloned.1.call-done, f32[1024]{0:T(1024)S(1)} %get-tuple-element.51, f32[1024]{0:T(1024)S(1)} %get-tuple-element.52, ...), kind=kOutput, calls=%fused_computation.190 | convolution fusion | flops 8597273600 | bytes 25190400 | tf_op jit(solution)/shard_map/dot_general | solution.py:26
  279.7 9.7 %convolution_convert_fusion.1 = bf16[4096,1024]{1,0:T(8,128)(2,1)S(1)} fusion(bf16[1024,4096]{1,0:T(8,128)(2,1)S(1)} %bitcast.331, bf16[1024,1024]{1,0:T(8,128)(2,1)S(1)} %get-tuple-element.29), kind=kOutput, calls=%fused_computation.23 | convolution fusion | flops 8594128896 | bytes 18874368 | tf_op jit(solution)/shard_map/dot_general | solution.py:30
  294.2 23.9 %fusion.59 = (bf16[4096]{0:T(1024)(128)(2,1)S(1)}, bf16[1024,4096]{1,0:T(8,128)(2,1)}) fusion(f32[1024,4096]{1,0:T(8,128)} %get-tuple-element.75, f32[1024,4096]{1,0:T(8,128)} %get-tuple-element.86, f32[4096]{0:T(1024)S(1)} %reshape.508, bf16[1024,1024]{1,0:T(8,128)(2,1)S(1)} %get-tuple-element.29, bf16[4096,1024]{1,0:T(8,128)(2,1)} %all-gather.8.cloned.1.call-done), kind=kOutput, calls=%fused_computation.182 | convolution fusion | flops 8657039360 | bytes 52453376 | tf_op jit(solution)/shard_map/dot_general | solution.py:36
  318.1 5.6 fusion.7
  325.9 15.2 %convolution_convert_fusion = bf16[1024,4096]{1,0:T(8,128)(2,1)} fusion(bf16[1024,4096]{1,0:T(8,128)(2,1)} %get-tuple-element.31, f32[1024,1024]{1,0:T(8,128)S(1)} %copy-done.4, f32[1024]{0:T(1024)S(1)} %get-tuple-element.51, f32[1024]{0:T(1024)S(1)} %get-tuple-element.52, f32[1024]{0:T(1024)S(1)} %fusion.53, f32[1024]{0:T(1024)S(1)} %broadcast_multiply_fusion.1), kind=kOutput, calls=%fused_computation.22 | convolution fusion | flops 8599371776 | bytes 20987904 | tf_op jit(solution)/shard_map/dot_general | solution.py:30
  341.1 15.3 %add_add_fusion.5 = f32[1024,1024]{1,0:T(8,128)} fusion(f32[1024,1024]{1,0:T(8,128)S(1)} %copy-done.13, f32[1024]{0:T(1024)S(1)} %negate_multiply_fusion.2, bf16[1024,4096]{1,0:T(8,128)(2,1)} %get-tuple-element.31, bf16[1024,4096]{1,0:T(8,128)(2,1)} %all-gather.6.cloned.1.call-done), kind=kOutput, calls=%fused_computation.54 | convolution fusion | flops 8592031744 | bytes 25169920 | tf_op jit(solution)/shard_map/dot_general | solution.py:36
  356.5 15.3 %collective-permute-done.1 = bf16[4,256,1024]{2,1,0:T(8,128)(2,1)S(1)} collective-permute-done((bf16[4,256,1024]{2,1,0:T(8,128)(2,1)S(1)}, bf16[4,256,1024]{2,1,0:T(8,128)(2,1)S(1)}, u32[]{:S(2)}, u32[]{:S(2)}) %collective-permute-start.1) | collective-permute-done | bytes 2097184 | tf_op jit(solution)/shard_map/ppermute | solution.py:170
  372.8 5.4 dynamic-slice_bitcast_fusion
  379.9 5.0 multiply_reduce_fusion
  389.7 3.8 convolution_convert_fusion.2
  393.5 4.1 convolution_convert_fusion.3.grad_ref
  397.6 6.4 collective-permute-done.3
  404.4 4.1 fusion.6
  426.2 13.7 %collective-permute-done.4 = bf16[1,256,1024]{2,1,0:T(8,128)(2,1)S(1)} collective-permute-done((bf16[1,256,1024]{2,1,0:T(8,128)(2,1)}, bf16[1,256,1024]{2,1,0:T(8,128)(2,1)S(1)}, u32[]{:S(2)}, u32[]{:S(2)}) %collective-permute-start.4) | collective-permute-done | bytes 524320 | tf_op jit(solution)/shard_map/ppermute | solution.py:170
  441.9 45.8 %shard_map.272 = bf16[3,1024,1024]{2,1,0:T(8,128)(2,1)S(1)} custom-call(s32[2,512,1]{2,1,0:T(8,128)S(1)} %copy.163.seg_col, s32[2,1,512]{2,1,0:T(1,128)S(1)} %broadcast_in_dim.60.seg_row, bf16[1024,3072]{1,0:T(8,128)(2,1)} %copy-done, bf16[1024,3072]{1,0:T(8,128)(2,1)} %copy-done, bf16[1024,3072]{1,0:T(8,128)(2,1)} %copy-done, ...), custom_call_target="tpu_custom_call" | custom-call | flops 10737418240 | bytes 14680064 | tf_op jit(solution)/shard_map/pallas_call | solution.py:133
  489.1 3.7 fusion.16
  494.4 9.3 %convert_bitcast_fusion = bf16[1024,3072]{1,0:T(8,128)(2,1)} fusion(bf16[1024,1024]{1,0:T(8,128)(2,1)S(1)} %bitcast.328, bf16[1024,1024]{1,0:T(8,128)(2,1)S(1)} %get-tuple-element.79, bf16[1024,1024]{1,0:T(8,128)(2,1)S(1)} %get-tuple-element.80, bf16[1024,1024]{1,0:T(8,128)(2,1)S(1)} %get-tuple-element.78), kind=kOutput, calls=%fused_computation.26 | convolution fusion | flops 6464471040 | bytes 14680064 | tf_op jit(solution)/shard_map/dot_general | solution.py:30
  523.4 12.2 %add_add_fusion.4 = f32[1024,1024]{1,0:T(8,128)} fusion(f32[1024,1024]{1,0:T(8,128)S(1)} %copy-done.8, f32[1024]{0:T(1024)S(1)} %negate_multiply_fusion.1, bf16[1024,4224]{1,0:T(8,128)(2,1)} %all-gather.4.cloned.1.call-done, bf16[1024,1024]{1,0:T(8,128)(2,1)} %copy-done.20, bf16[1024,1024]{1,0:T(8,128)(2,1)} %copy-done.21, bf16[1024,1024]{1,0:T(8,128)(2,1)} %copy-done.19), kind=kOutput, calls=%fused_computation.52 | convolution fusion | flops 6463422464 | bytes 20975616 | tf_op jit(solution)/shard_map/dot_general | solution.py:36
  537.9 18.1 %collective-permute-done.19 = bf16[4,32,128]{2,1,0:T(8,128)(2,1)S(1)} collective-permute-done((bf16[4,32,128]{2,1,0:T(8,128)(2,1)S(1)}, bf16[4,32,128]{2,1,0:T(8,128)(2,1)S(1)}, u32[]{:S(2)}, u32[]{:S(2)}) %collective-permute-start.19) | collective-permute-done | bytes 32800 | tf_op jit(solution)/shard_map/ppermute | solution.py:170
  563.0 6.9 %collective-permute-done.23 = bf16[4,32,1024]{2,1,0:T(8,128)(2,1)S(1)} collective-permute-done((bf16[4,32,1024]{2,1,0:T(8,128)(2,1)S(1)}, bf16[4,32,1024]{2,1,0:T(8,128)(2,1)S(1)}, u32[]{:S(2)}, u32[]{:S(2)}) %collective-permute-start.23) | collective-permute-done | bytes 262176 | tf_op jit(solution)/shard_map/ppermute | solution.py:170
  593.1 17.1 %collective-permute-done.27 = bf16[1,64,4096]{2,1,0:T(8,128)(2,1)S(1)} collective-permute-done((bf16[1,64,4096]{2,1,0:T(8,128)(2,1)S(1)}, bf16[1,64,4096]{2,1,0:T(8,128)(2,1)S(1)}, u32[]{:S(2)}, u32[]{:S(2)}) %collective-permute-start.27) | collective-permute-done | bytes 524320 | tf_op jit(solution)/shard_map/ppermute | solution.py:170
  613.0 5.6 collective-permute-done.28
  620.3 12.5 %collective-permute-done.8 = bf16[8,32,1536]{2,1,0:T(8,128)(2,1)S(1)} collective-permute-done((bf16[8,32,1536]{2,1,0:T(8,128)(2,1)S(1)}, bf16[8,32,1536]{2,1,0:T(8,128)(2,1)S(1)}, u32[]{:S(2)}, u32[]{:S(2)}) %collective-permute-start.8) | collective-permute-done | bytes 786464 | tf_op jit(solution)/shard_map/ppermute | solution.py:170
  633.8 6.5 collective-permute-done.14
  644.3 12.4 %collective-permute-done.15 = bf16[1,64,1536]{2,1,0:T(8,128)(2,1)S(1)} collective-permute-done((bf16[1,64,1536]{2,1,0:T(8,128)(2,1)S(1)}, bf16[1,64,1536]{2,1,0:T(8,128)(2,1)S(1)}, u32[]{:S(2)}, u32[]{:S(2)}) %collective-permute-start.15) | collective-permute-done | bytes 196640 | tf_op jit(solution)/shard_map/ppermute | solution.py:170
  (245 shorter events, 135.7 us)
Async XLA Ops:
  7.2 89.9 %all-gather.4.cloned.1.call-start = ((), (), s32[]{:S(2)}) async-start(), calls=%async_computation | async-start | bytes 8921088 | tf_op jit(solution)/shard_map/all_gather | solution.py:210
  15.8 160.3 %all-gather.6.cloned.1.call-start = ((), (), s32[]{:S(2)}) async-start(), calls=%async_computation.1 | async-start | bytes 8650752 | tf_op jit(solution)/shard_map/all_gather | solution.py:213
  16.6 238.6 %all-gather.8.cloned.1.call-start = ((), (), s32[]{:S(2)}) async-start(), calls=%async_computation.2 | async-start | bytes 8650752 | tf_op jit(solution)/shard_map/all_gather | solution.py:214
  293.9 24.2 %collective-permute-start = (bf16[16,128,1024]{2,1,0:T(8,128)(2,1)}, bf16[16,128,1024]{2,1,0:T(8,128)(2,1)}, u32[]{:S(2)}, u32[]{:S(2)}) collective-permute-start(bf16[16,128,1024]{2,1,0:T(8,128)(2,1)} %dynamic-slice_bitcast_fusion.1), channel_id=1, source_target_pairs={{0,1},{1,0},{2,3},{3,2},{4,5},{5,4},{6,7},{7,6},{8,9},{9,8},{10,11... | collective-permute-start | bytes 12582920 | tf_op jit(solution)/shard_map/ppermute | solution.py:170
  323.9 47.9 %collective-permute-start.1 = (bf16[4,256,1024]{2,1,0:T(8,128)(2,1)S(1)}, bf16[4,256,1024]{2,1,0:T(8,128)(2,1)S(1)}, u32[]{:S(2)}, u32[]{:S(2)}) collective-permute-start(bf16[4,256,1024]{2,1,0:T(8,128)(2,1)S(1)} %dynamic-slice_bitcast_fusion.3), channel_id=1, source_target_pairs={{0,4},{4,0},{8,12},{12,8},{16,20},{20,16},{24,28},{28,24},{1,5},{5... | collective-permute-start | bytes 6291464 | tf_op jit(solution)/shard_map/ppermute | solution.py:170
  378.2 26.2 %collective-permute-start.2 = (bf16[16,32,4096]{2,1,0:T(8,128)(2,1)}, bf16[16,32,4096]{2,1,0:T(8,128)(2,1)}, u32[]{:S(2)}, u32[]{:S(2)}) collective-permute-start(bf16[16,32,4096]{2,1,0:T(8,128)(2,1)} %dynamic-slice_bitcast_fusion), channel_id=1, source_target_pairs={{0,1},{1,0},{2,3},{3,2},{4,5},{5,4},{6,7},{7,6},{8,9},{9,8},{10,11... | collective-permute-start | bytes 12582920 | tf_op jit(solution)/shard_map/ppermute | solution.py:170
  378.3 25.6 %collective-permute-start.3 = (bf16[4,128,1024]{2,1,0:T(8,128)(2,1)S(1)}, bf16[4,128,1024]{2,1,0:T(8,128)(2,1)S(1)}, u32[]{:S(2)}, u32[]{:S(2)}) collective-permute-start(bf16[4,128,1024]{2,1,0:T(8,128)(2,1)S(1)} %dynamic-slice_bitcast_fusion.8), channel_id=1, source_target_pairs={{0,2},{1,3},{2,0},{3,1},{4,6},{5,7},{6,4},{7,5},{8,10},{9,11},{10,... | collective-permute-start | bytes 3145736 | tf_op jit(solution)/shard_map/ppermute | solution.py:170
  411.9 77.2 %collective-permute-start.5 = (bf16[8,32,4096]{2,1,0:T(8,128)(2,1)}, bf16[8,32,4096]{2,1,0:T(8,128)(2,1)}, u32[]{:S(2)}, u32[]{:S(2)}) collective-permute-start(bf16[8,32,4096]{2,1,0:T(8,128)(2,1)} %dynamic-slice_bitcast_fusion.2), channel_id=1, source_target_pairs={{0,2},{1,3},{2,0},{3,1},{4,6},{5,7},{6,4},{7,5},{8,10},{9,11},{10,... | collective-permute-start | bytes 6291464 | tf_op jit(solution)/shard_map/ppermute | solution.py:170
  414.2 25.6 %collective-permute-start.4 = (bf16[1,256,1024]{2,1,0:T(8,128)(2,1)}, bf16[1,256,1024]{2,1,0:T(8,128)(2,1)S(1)}, u32[]{:S(2)}, u32[]{:S(2)}) collective-permute-start(bf16[1,256,1024]{2,1,0:T(8,128)(2,1)} %dynamic-slice_bitcast_fusion.13), channel_id=1, source_target_pairs={{0,16},{4,20},{8,24},{12,28},{16,0},{20,4},{24,8},{28,12},{1,17},{... | collective-permute-start | bytes 1572872 | tf_op jit(solution)/shard_map/ppermute | solution.py:170
  426.1 61.6 %collective-permute-start.6 = (bf16[16,32,1024]{2,1,0:T(8,128)(2,1)S(1)}, bf16[16,32,1024]{2,1,0:T(8,128)(2,1)S(1)}, u32[]{:S(2)}, u32[]{:S(2)}) collective-permute-start(bf16[16,32,1024]{2,1,0:T(8,128)(2,1)S(1)} %dynamic-slice_bitcast_fusion.7), channel_id=1, source_target_pairs={{0,1},{1,0},{2,3},{3,2},{4,5},{5,4},{6,7},{7,6},{8,9},{9,8},{10,11... | collective-permute-start | bytes 3145736 | tf_op jit(solution)/shard_map/ppermute | solution.py:170
  510.0 80.6 %collective-permute-start.12 = (bf16[16,32,1536]{2,1,0:T(8,128)(2,1)}, bf16[16,32,1536]{2,1,0:T(8,128)(2,1)}, u32[]{:S(2)}, u32[]{:S(2)}) collective-permute-start(bf16[16,32,1536]{2,1,0:T(8,128)(2,1)} %dynamic-slice_bitcast_fusion.4), channel_id=1, source_target_pairs={{0,1},{1,0},{2,3},{3,2},{4,5},{5,4},{6,7},{7,6},{8,9},{9,8},{10,11... | collective-permute-start | bytes 4718600 | tf_op jit(solution)/shard_map/ppermute | solution.py:170
  511.2 99.2 %collective-permute-start.7 = (bf16[16,32,1536]{2,1,0:T(8,128)(2,1)}, bf16[16,32,1536]{2,1,0:T(8,128)(2,1)}, u32[]{:S(2)}, u32[]{:S(2)}) collective-permute-start(bf16[16,32,1536]{2,1,0:T(8,128)(2,1)} %dynamic-slice_bitcast_fusion.5), channel_id=1, source_target_pairs={{0,1},{1,0},{2,3},{3,2},{4,5},{5,4},{6,7},{7,6},{8,9},{9,8},{10,11... | collective-permute-start | bytes 4718600 | tf_op jit(solution)/shard_map/ppermute | solution.py:170
  516.9 5.7 collective-permute-start.17
  518.3 37.8 %collective-permute-start.22 = (bf16[4,64,1024]{2,1,0:T(8,128)(2,1)S(1)}, bf16[4,64,1024]{2,1,0:T(8,128)(2,1)S(1)}, u32[]{:S(2)}, u32[]{:S(2)}) collective-permute-start(bf16[4,64,1024]{2,1,0:T(8,128)(2,1)S(1)} %dynamic-slice_bitcast_fusion.12), channel_id=1, source_target_pairs={{0,4},{4,0},{8,12},{12,8},{16,20},{20,16},{24,28},{28,24},{1,5},{5... | collective-permute-start | bytes 1572872 | tf_op jit(solution)/shard_map/ppermute | solution.py:170
  521.2 64.9 %collective-permute-start.26 = (bf16[4,32,4096]{2,1,0:T(8,128)(2,1)}, bf16[4,32,4096]{2,1,0:T(8,128)(2,1)}, u32[]{:S(2)}, u32[]{:S(2)}) collective-permute-start(bf16[4,32,4096]{2,1,0:T(8,128)(2,1)} %dynamic-slice_bitcast_fusion.6), channel_id=1, source_target_pairs={{0,4},{4,0},{8,12},{12,8},{16,20},{20,16},{24,28},{28,24},{1,5},{5... | collective-permute-start | bytes 3145736 | tf_op jit(solution)/shard_map/ppermute | solution.py:170
  522.8 12.9 %collective-permute-start.18 = (bf16[8,32,128]{2,1,0:T(8,128)(2,1)S(1)}, bf16[8,32,128]{2,1,0:T(8,128)(2,1)S(1)}, u32[]{:S(2)}, u32[]{:S(2)}) collective-permute-start(bf16[8,32,128]{2,1,0:T(8,128)(2,1)S(1)} %dynamic-slice_bitcast_fusion.26), channel_id=1, source_target_pairs={{0,2},{1,3},{2,0},{3,1},{4,6},{5,7},{6,4},{7,5},{8,10},{9,11},{10,... | collective-permute-start | bytes 196616 | tf_op jit(solution)/shard_map/ppermute | solution.py:170
  535.7 20.3 %collective-permute-start.19 = (bf16[4,32,128]{2,1,0:T(8,128)(2,1)S(1)}, bf16[4,32,128]{2,1,0:T(8,128)(2,1)S(1)}, u32[]{:S(2)}, u32[]{:S(2)}) collective-permute-start(bf16[4,32,128]{2,1,0:T(8,128)(2,1)S(1)} %dynamic-slice_bitcast_fusion.27), channel_id=1, source_target_pairs={{0,4},{4,0},{8,12},{12,8},{16,20},{20,16},{24,28},{28,24},{1,5},{5... | collective-permute-start | bytes 98312 | tf_op jit(solution)/shard_map/ppermute | solution.py:170
  556.0 27.2 %collective-permute-start.29 = (bf16[1,128,1024]{2,1,0:T(8,128)(2,1)}, bf16[1,128,1024]{2,1,0:T(8,128)(2,1)}, u32[]{:S(2)}, u32[]{:S(2)}) collective-permute-start(bf16[1,128,1024]{2,1,0:T(8,128)(2,1)} %dynamic-slice_bitcast_fusion.16), channel_id=1, source_target_pairs={{0,8},{4,12},{8,0},{12,4},{16,24},{20,28},{24,16},{28,20},{1,9},{5... | collective-permute-start | bytes 786440 | tf_op jit(solution)/shard_map/ppermute | solution.py:170
  556.0 6.3 collective-permute-start.20
  562.4 7.5 %collective-permute-start.23 = (bf16[4,32,1024]{2,1,0:T(8,128)(2,1)S(1)}, bf16[4,32,1024]{2,1,0:T(8,128)(2,1)S(1)}, u32[]{:S(2)}, u32[]{:S(2)}) collective-permute-start(bf16[4,32,1024]{2,1,0:T(8,128)(2,1)S(1)} %dynamic-slice_bitcast_fusion.18), channel_id=1, source_target_pairs={{0,2},{1,3},{2,0},{3,1},{4,6},{5,7},{6,4},{7,5},{8,10},{9,11},{10,... | collective-permute-start | bytes 786440 | tf_op jit(solution)/shard_map/ppermute | solution.py:170
  574.1 6.0 collective-permute-start.24
  581.0 4.4 collective-permute-start.25
  587.9 22.3 %collective-permute-start.27 = (bf16[1,64,4096]{2,1,0:T(8,128)(2,1)S(1)}, bf16[1,64,4096]{2,1,0:T(8,128)(2,1)S(1)}, u32[]{:S(2)}, u32[]{:S(2)}) collective-permute-start(bf16[1,64,4096]{2,1,0:T(8,128)(2,1)S(1)} %dynamic-slice_bitcast_fusion.11), channel_id=1, source_target_pairs={{0,16},{4,20},{8,24},{12,28},{16,0},{20,4},{24,8},{28,12},{1,17},{... | collective-permute-start | bytes 1572872 | tf_op jit(solution)/shard_map/ppermute | solution.py:170
  592.5 27.0 %collective-permute-start.13 = (bf16[4,64,1536]{2,1,0:T(8,128)(2,1)S(1)}, bf16[4,64,1536]{2,1,0:T(8,128)(2,1)S(1)}, u32[]{:S(2)}, u32[]{:S(2)}) collective-permute-start(bf16[4,64,1536]{2,1,0:T(8,128)(2,1)S(1)} %dynamic-slice_bitcast_fusion.9), channel_id=1, source_target_pairs={{0,4},{4,0},{8,12},{12,8},{16,20},{20,16},{24,28},{28,24},{1,5},{5... | collective-permute-start | bytes 2359304 | tf_op jit(solution)/shard_map/ppermute | solution.py:170
  610.4 8.2 %collective-permute-start.28 = (bf16[1,32,4096]{2,1,0:T(8,128)(2,1)S(1)}, bf16[1,32,4096]{2,1,0:T(8,128)(2,1)S(1)}, u32[]{:S(2)}, u32[]{:S(2)}) collective-permute-start(bf16[1,32,4096]{2,1,0:T(8,128)(2,1)S(1)} %dynamic-slice_bitcast_fusion.17), channel_id=1, source_target_pairs={{0,8},{4,12},{8,0},{12,4},{16,24},{20,28},{24,16},{28,20},{1,9},{5... | collective-permute-start | bytes 786440 | tf_op jit(solution)/shard_map/ppermute | solution.py:170
  612.4 20.5 %collective-permute-start.8 = (bf16[8,32,1536]{2,1,0:T(8,128)(2,1)S(1)}, bf16[8,32,1536]{2,1,0:T(8,128)(2,1)S(1)}, u32[]{:S(2)}, u32[]{:S(2)}) collective-permute-start(bf16[8,32,1536]{2,1,0:T(8,128)(2,1)S(1)} %dynamic-slice_bitcast_fusion.10), channel_id=1, source_target_pairs={{0,2},{1,3},{2,0},{3,1},{4,6},{5,7},{6,4},{7,5},{8,10},{9,11},{10,... | collective-permute-start | bytes 2359304 | tf_op jit(solution)/shard_map/ppermute | solution.py:170
  619.7 20.6 %collective-permute-start.14 = (bf16[4,32,1536]{2,1,0:T(8,128)(2,1)S(1)}, bf16[4,32,1536]{2,1,0:T(8,128)(2,1)S(1)}, u32[]{:S(2)}, u32[]{:S(2)}) collective-permute-start(bf16[4,32,1536]{2,1,0:T(8,128)(2,1)S(1)} %dynamic-slice_bitcast_fusion.14), channel_id=1, source_target_pairs={{0,2},{1,3},{2,0},{3,1},{4,6},{5,7},{6,4},{7,5},{8,10},{9,11},{10,... | collective-permute-start | bytes 1179656 | tf_op jit(solution)/shard_map/ppermute | solution.py:170
  633.2 9.5 %collective-permute-start.9 = (bf16[4,32,1536]{2,1,0:T(8,128)(2,1)S(1)}, bf16[4,32,1536]{2,1,0:T(8,128)(2,1)S(1)}, u32[]{:S(2)}, u32[]{:S(2)}) collective-permute-start(bf16[4,32,1536]{2,1,0:T(8,128)(2,1)S(1)} %dynamic-slice_bitcast_fusion.15), channel_id=1, source_target_pairs={{0,4},{4,0},{8,12},{12,8},{16,20},{20,16},{24,28},{28,24},{1,5},{5... | collective-permute-start | bytes 1179656 | tf_op jit(solution)/shard_map/ppermute | solution.py:170
  640.4 16.3 %collective-permute-start.15 = (bf16[1,64,1536]{2,1,0:T(8,128)(2,1)S(1)}, bf16[1,64,1536]{2,1,0:T(8,128)(2,1)S(1)}, u32[]{:S(2)}, u32[]{:S(2)}) collective-permute-start(bf16[1,64,1536]{2,1,0:T(8,128)(2,1)S(1)} %dynamic-slice_bitcast_fusion.19), channel_id=1, source_target_pairs={{0,16},{4,20},{8,24},{12,28},{16,0},{20,4},{24,8},{28,12},{1,17},{... | collective-permute-start | bytes 589832 | tf_op jit(solution)/shard_map/ppermute | solution.py:170
  642.8 17.3 %collective-permute-start.10 = (bf16[1,64,1536]{2,1,0:T(8,128)(2,1)S(1)}, bf16[1,64,1536]{2,1,0:T(8,128)(2,1)S(1)}, u32[]{:S(2)}, u32[]{:S(2)}) collective-permute-start(bf16[1,64,1536]{2,1,0:T(8,128)(2,1)S(1)} %dynamic-slice_bitcast_fusion.20), channel_id=1, source_target_pairs={{0,16},{4,20},{8,24},{12,28},{16,0},{20,4},{24,8},{28,12},{1,17},{... | collective-permute-start | bytes 589832 | tf_op jit(solution)/shard_map/ppermute | solution.py:170
  656.8 5.5 collective-permute-start.16
  660.2 4.7 collective-permute-start.11
  (39 other events, 551.5 us)
Sparse Core Ops, SparseCore 0:
  16.0 81.0 all-gather.3
  99.9 76.1 all-gather.5
  179.0 76.1 all-gather.7
